TPU v7x, 128 devices: a whole 4x4x4 slice. The times are simulated.
128 devices in a mesh: ctx: 32 (over x, y, core), head: 4 (over z).
Axes of the slice: x: 4, y: 4, z: 4, core: 2. Of those that a mesh axis runs over, the one named last changes fastest.
Arguments:
- queries: bfloat16 [24576, 2048], P(('ctx', 'head')), may hold values from -9 to 9
- keys: bfloat16 [24576, 2048], P(('ctx', 'head')), may hold values from -9 to 9
- values: bfloat16 [24576, 2048], P(('ctx', 'head')), may hold values from -12 to 12
- grad_out: bfloat16 [24576, 2048], P(('ctx', 'head')), may hold values from -6 to 6
- pattern: int32 [192, 16], replicated, may hold values from -1 to 191, as said below
Outputs:
- attn_out: bfloat16 [24576, 2048], P(('ctx', 'head'))
- grad_query: bfloat16 [24576, 2048], P(('ctx', 'head'))
- grad_key: bfloat16 [24576, 2048], P(('ctx', 'head'))
- grad_value: bfloat16 [24576, 2048], P(('ctx', 'head'))
Inputs may be any that keep to these rules, and one draw needn't show every extreme that they name: `pattern`: row b: entries 0 to 3 are the blocks b - 3 to b in order, -1 where such a number is negative; the remaining entries are, ascending, some of the blocks c <= b - 4 whose remainder modulo 16 equals one phase shared by all rows (each row its own subset, always holding the smallest such block where one exists), followed by -1.
All inputs are finite; a program needn't handle non-finite values.
Results may differ from a plain program's by a relative error of at most 0.015.
Values may be sent and summed in bfloat16 or wider, within the bound.
A program may use at most 128 MiB of HBM per device.

v0:
```python
import math

import jax
import jax.numpy as jnp
from jax import lax
from jax.sharding import PartitionSpec as P

HEAD_DIM = 128
HEAD_DEV = 4
BLOCK = 128
LOCAL = 4
STRIDE = 16
TOK_DEV = 768


def shifted(value, axis, steps):
    count = lax.axis_size(axis)
    first, last = (max(0, -steps), min(count, count - steps))
    return lax.ppermute(value, axis, [(source, source + steps) for source in range(first, last)])


def per_device(queries, keys, values, grad_out, pattern):
    query_here, key_here, value_here, grad_here = (
        lax.all_to_all(queries, "head", split_axis=1, concat_axis=0, tiled=True),
        lax.all_to_all(keys, "head", split_axis=1, concat_axis=0, tiled=True),
        lax.all_to_all(values, "head", split_axis=1, concat_axis=0, tiled=True),
        lax.all_to_all(grad_out, "head", split_axis=1, concat_axis=0, tiled=True),
    )
    device = lax.axis_index("ctx")
    cycle_size = lax.axis_size("ctx")
    blocks_here = TOK_DEV // BLOCK
    block_total = pattern.shape[0]
    strided_count = block_total // STRIDE
    owned_count = (blocks_here + STRIDE - 1) // STRIDE
    features = HEAD_DEV * HEAD_DIM
    score_scale = 1.0 / math.sqrt(HEAD_DIM)
    edge_rows = (LOCAL - 1) * BLOCK
    stride_phase = pattern[block_total - 1, LOCAL] % STRIDE
    first_local = jnp.mod(stride_phase - device * blocks_here, STRIDE)
    own_local = first_local + STRIDE * jnp.arange(owned_count, dtype=jnp.int32)
    own_valid = own_local < blocks_here
    own_safe = jnp.where(own_valid, own_local, 0)
    key_blocks = key_here.reshape(blocks_here, BLOCK, features)
    value_blocks = value_here.reshape(blocks_here, BLOCK, features)
    offer_keys = jnp.where(own_valid[:, None, None], key_blocks[own_safe], 0)
    offer_values = jnp.where(own_valid[:, None, None], value_blocks[own_safe], 0)
    pool_ids = stride_phase + STRIDE * jnp.arange(strided_count, dtype=jnp.int32)
    pool_owner = pool_ids // blocks_here
    slot_within = (pool_ids - pool_owner * blocks_here) // STRIDE
    pool_slots = pool_owner * owned_count + slot_within
    all_keys, all_values = (
        lax.all_gather(
            offer_keys.reshape(owned_count * BLOCK, features), "ctx", axis=0, tiled=True
        ),
        lax.all_gather(
            offer_values.reshape(owned_count * BLOCK, features), "ctx", axis=0, tiled=True
        ),
    )
    pool_keys = all_keys.reshape(cycle_size * owned_count, BLOCK, features)[pool_slots]
    pool_values = all_values.reshape(cycle_size * owned_count, BLOCK, features)[pool_slots]
    before_keys, before_values = shifted(
        (key_here[TOK_DEV - edge_rows :], value_here[TOK_DEV - edge_rows :]), "ctx", 1
    )
    window_keys = jnp.concatenate([before_keys, key_here], 0).reshape(
        edge_rows + TOK_DEV, HEAD_DEV, HEAD_DIM
    )
    window_values = jnp.concatenate([before_values, value_here], 0).reshape(
        edge_rows + TOK_DEV, HEAD_DEV, HEAD_DIM
    )
    pool_keys3 = pool_keys.reshape(strided_count * BLOCK, HEAD_DEV, HEAD_DIM)
    pool_values3 = pool_values.reshape(strided_count * BLOCK, HEAD_DEV, HEAD_DIM)
    my_rows = lax.dynamic_slice_in_dim(pattern, device * blocks_here, blocks_here, 0)
    span_rows = LOCAL * BLOCK
    key_place = jnp.arange(span_rows)
    query_place = jnp.arange(BLOCK)
    last_start = (LOCAL - 1) * BLOCK
    causal = (key_place[None, :] < last_start) | (
        key_place[None, :] - last_start <= query_place[:, None]
    )

    def attend_block(totals, operands):
        key_ext, value_ext, key_pool, value_pool = totals
        block_index, query_block, grad_block, pattern_row = operands
        near_keys = lax.dynamic_slice_in_dim(window_keys, block_index * BLOCK, span_rows, 0)
        near_values = lax.dynamic_slice_in_dim(window_values, block_index * BLOCK, span_rows, 0)
        joined_keys = jnp.concatenate([near_keys, pool_keys3], 0)
        joined_values = jnp.concatenate([near_values, pool_values3], 0)
        near_allowed = jnp.repeat(pattern_row[:LOCAL] >= 0, BLOCK)
        far_allowed = jnp.repeat(
            jnp.any(pattern_row[LOCAL:][None, :] == pool_ids[:, None], axis=1), BLOCK
        )
        allowed = jnp.concatenate(
            [
                causal & near_allowed[None, :],
                jnp.broadcast_to(far_allowed[None, :], (BLOCK, strided_count * BLOCK)),
            ],
            1,
        )
        scores = (
            jnp.einsum("qhd,khd->hqk", query_block, joined_keys, preferred_element_type=jnp.float32)
            * score_scale
        )
        masked = jnp.where(allowed[None], scores, -jnp.inf)
        row_top = jnp.max(masked, axis=2, keepdims=True)
        exponent = jnp.exp(masked - row_top)
        weights_wide = exponent / jnp.sum(exponent, axis=2, keepdims=True)
        weights = weights_wide.astype(jnp.bfloat16)
        output_wide = jnp.einsum(
            "hqk,khd->qhd", weights, joined_values, preferred_element_type=jnp.float32
        )
        grad_weights = jnp.einsum(
            "qhd,khd->hqk", grad_block, joined_values, preferred_element_type=jnp.float32
        )
        row_delta = jnp.sum(grad_block.astype(jnp.float32) * output_wide, axis=2).T[:, :, None]
        grad_scores = (score_scale * weights_wide * (grad_weights - row_delta)).astype(jnp.bfloat16)
        grad_query = jnp.einsum(
            "hqk,khd->qhd", grad_scores, joined_keys, preferred_element_type=jnp.float32
        )
        key_terms = jnp.einsum(
            "hqk,qhd->khd", grad_scores, query_block, preferred_element_type=jnp.float32
        )
        value_terms = jnp.einsum(
            "hqk,qhd->khd", weights, grad_block, preferred_element_type=jnp.float32
        )
        start_row = block_index * BLOCK
        key_ext = lax.dynamic_update_slice_in_dim(
            key_ext,
            lax.dynamic_slice_in_dim(key_ext, start_row, span_rows, 0) + key_terms[:span_rows],
            start_row,
            0,
        )
        value_ext = lax.dynamic_update_slice_in_dim(
            value_ext,
            lax.dynamic_slice_in_dim(value_ext, start_row, span_rows, 0) + value_terms[:span_rows],
            start_row,
            0,
        )
        key_pool = key_pool + key_terms[span_rows:]
        value_pool = value_pool + value_terms[span_rows:]
        return (
            (key_ext, value_ext, key_pool, value_pool),
            (output_wide.astype(jnp.bfloat16), grad_query.astype(jnp.bfloat16)),
        )

    ext_zero = jnp.zeros((edge_rows + TOK_DEV, HEAD_DEV, HEAD_DIM), jnp.float32)
    pool_zero = jnp.zeros((strided_count * BLOCK, HEAD_DEV, HEAD_DIM), jnp.float32)
    operands = (
        jnp.arange(blocks_here, dtype=jnp.int32),
        query_here.reshape(blocks_here, BLOCK, HEAD_DEV, HEAD_DIM),
        grad_here.reshape(blocks_here, BLOCK, HEAD_DEV, HEAD_DIM),
        my_rows,
    )
    (key_ext, value_ext, key_pool, value_pool), (outputs, query_grads) = lax.scan(
        attend_block, (ext_zero, ext_zero, pool_zero, pool_zero), operands
    )
    key_ext = key_ext.reshape(edge_rows + TOK_DEV, features)
    value_ext = value_ext.reshape(edge_rows + TOK_DEV, features)
    back_keys, back_values = (
        shifted(key_ext[:edge_rows].astype(jnp.bfloat16), "ctx", -1).astype(jnp.float32),
        shifted(value_ext[:edge_rows].astype(jnp.bfloat16), "ctx", -1).astype(jnp.float32),
    )
    own_keys = key_ext[edge_rows:] + jnp.pad(back_keys, ((TOK_DEV - edge_rows, 0), (0, 0)))
    own_values = value_ext[edge_rows:] + jnp.pad(back_values, ((TOK_DEV - edge_rows, 0), (0, 0)))
    pool_key_grads = key_pool.reshape(strided_count, BLOCK, features)
    pool_value_grads = value_pool.reshape(strided_count, BLOCK, features)
    slot_keys = (
        jnp.zeros((cycle_size * owned_count, BLOCK, features), jnp.float32)
        .at[pool_slots]
        .set(pool_key_grads)
    )
    slot_values = (
        jnp.zeros((cycle_size * owned_count, BLOCK, features), jnp.float32)
        .at[pool_slots]
        .set(pool_value_grads)
    )
    mine_keys, mine_values = (
        lax.psum_scatter(
            slot_keys.reshape(cycle_size * owned_count * BLOCK, features).astype(jnp.bfloat16),
            "ctx",
            scatter_dimension=0,
            tiled=True,
        ).astype(jnp.float32),
        lax.psum_scatter(
            slot_values.reshape(cycle_size * owned_count * BLOCK, features).astype(jnp.bfloat16),
            "ctx",
            scatter_dimension=0,
            tiled=True,
        ).astype(jnp.float32),
    )
    mine_keys = mine_keys.reshape(owned_count, BLOCK, features)
    mine_values = mine_values.reshape(owned_count, BLOCK, features)
    own_keys = (
        own_keys.reshape(blocks_here, BLOCK, features)
        .at[own_safe]
        .add(jnp.where(own_valid[:, None, None], mine_keys, 0.0))
    )
    own_values = (
        own_values.reshape(blocks_here, BLOCK, features)
        .at[own_safe]
        .add(jnp.where(own_valid[:, None, None], mine_values, 0.0))
    )
    attn_local = outputs.reshape(TOK_DEV, features)
    query_local = query_grads.reshape(TOK_DEV, features)
    key_local = own_keys.reshape(TOK_DEV, features).astype(jnp.bfloat16)
    value_local = own_values.reshape(TOK_DEV, features).astype(jnp.bfloat16)
    attn_out, grad_query, grad_key, grad_value = (
        lax.all_to_all(attn_local, "head", split_axis=0, concat_axis=1, tiled=True),
        lax.all_to_all(query_local, "head", split_axis=0, concat_axis=1, tiled=True),
        lax.all_to_all(key_local, "head", split_axis=0, concat_axis=1, tiled=True),
        lax.all_to_all(value_local, "head", split_axis=0, concat_axis=1, tiled=True),
    )
    return (attn_out, grad_query, grad_key, grad_value)


def solution(mesh):
    placed = (
        P(("ctx", "head"), None),
        P(("ctx", "head"), None),
        P(("ctx", "head"), None),
        P(("ctx", "head"), None),
        P(),
    )
    return jax.shard_map(
        per_device,
        mesh=mesh,
        in_specs=placed,
        out_specs=(
            P(("ctx", "head"), None),
            P(("ctx", "head"), None),
            P(("ctx", "head"), None),
            P(("ctx", "head"), None),
        ),
        check_vma=False,
    )
```

profile of v0, /device:TPU:1, one launch (start us, length us, event | category | flops | bytes accessed | tf_op | source)
XLA Modules:
  0.0 576.3 jit_solution(18047088099131019259)
XLA Ops:
  9.3 5.9 %all-to-all-start.1 = ((bf16[192,4,512]{2,0,1:T(8,128)(2,1)}), bf16[192,4,512]{2,0,1:T(8,128)(2,1)S(1)}, u32[]{:S(2)}, u32[]{:S(2)}) async-start(bf16[192,4,512]{2,0,1:T(8,128)(2,1)} %bitcast.108), calls=%async_computation.1 | async-start | bytes 1572864 | tf_op jit(solution)/shard_map/all_to_all | solution.py:25
  17.8 8.8 %all-to-all-done.1 = bf16[192,4,512]{2,0,1:T(8,128)(2,1)S(1)} async-done(((bf16[192,4,512]{2,0,1:T(8,128)(2,1)}), bf16[192,4,512]{2,0,1:T(8,128)(2,1)S(1)}, u32[]{:S(2)}, u32[]{:S(2)}) %all-to-all-start.1) | async-done | bytes 786464 | tf_op jit(solution)/shard_map/all_to_all | solution.py:25
  27.4 13.0 %all_to_all.134 = bf16[192,4,512]{2,0,1:T(8,128)(2,1)S(1)} all-to-all(bf16[192,4,512]{2,0,1:T(8,128)(2,1)S(1)} %bitcast.174), channel_id=1, replica_groups=mesh['ctx'=32,'head'=4] {'head'}, dimensions={1} | all-to-all | bytes 1572864 | tf_op jit(solution)/shard_map/all_to_all | solution.py:26
  46.5 8.2 %all-to-all-done = bf16[192,4,512]{2,0,1:T(8,128)(2,1)S(1)} async-done(((bf16[192,4,512]{2,0,1:T(8,128)(2,1)}), bf16[192,4,512]{2,0,1:T(8,128)(2,1)S(1)}, u32[]{:S(2)}, u32[]{:S(2)}) %all-to-all-start) | async-done | bytes 786464 | tf_op jit(solution)/shard_map/all_to_all | solution.py:24
  59.9 7.1 %collective-permute-start = (bf16[384,512]{1,0:T(8,128)(2,1)}, bf16[384,512]{1,0:T(8,128)(2,1)}, u32[]{:S(2)}, u32[]{:S(2)}) collective-permute-start(bf16[384,512]{1,0:T(8,128)(2,1)} %bitcast.2), channel_id=1, source_target_pairs={{0,4},{4,8},{8,12},{12,16},{16,20},{20,24},{24,28},{28,32},{32,36}... | collective-permute-start | bytes 1179656 | tf_op jit(solution)/shard_map/ppermute | solution.py:19
  78.4 4.9 pad_maximum_fusion
  83.3 5.7 pad_maximum_fusion.1
  89.0 4.1 gather_fusion
  96.9 25.3 %all-gather.7.cloned.1.call-done = bf16[1,4096,512]{2,1,0:T(8,128)(2,1)} async-done(((bf16[1,128,512]{2,1,0:T(8,128)(2,1)}), bf16[1,4096,512]{2,1,0:T(8,128)(2,1)}) %all-gather.7.cloned.1.call-update) | async-done | bytes 4194320 | tf_op jit(solution)/shard_map/all_gather | solution.py:55
  122.1 4.0 gather_fusion.1
  133.1 219.7 %while.25 = (s32[]{:T(128)}, f32[1152,4,128]{0,2,1:T(8,128)}, f32[1152,4,128]{0,2,1:T(8,128)}, f32[1536,4,128]{0,2,1:T(8,128)}, f32[1536,4,128]{0,2,1:T(8,128)},...) while((s32[]{:T(128)}, f32[1152,4,128]{0,2,1:T(8,128)}, ...), condition=%wide.region_5.6_spmd.clone, body=%wide.region_0.5_spmd.clone.sunk | while | flops 1626605312 | bytes 194795088 | solution.py:153
  234.0 3.6 fusion.56
  358.9 4.3 broadcast.237.clone
  363.3 6.2 %scatter_fusion = f32[32,128,512]{2,1,0:T(8,128)} fusion(f32[32,128,512]{2,1,0:T(8,128)} %broadcast.237.clone, s32[12]{0:T(128)S(1)} %fusion.22, f32[12,128,512]{2,1,0:T(8,128)S(1)} %copy-done.11), kind=kCustom, calls=%fused_computation.2 | custom fusion | bytes 9437232 | tf_op jit(solution)/shard_map/scatter | solution.py:169
  369.4 6.0 %convert_element_type.67 = bf16[32,128,512]{2,1,0:T(8,128)(2,1)} convert(f32[32,128,512]{2,1,0:T(8,128)} %scatter_fusion) | non-fusion elementwise | flops 2097152 | bytes 12582912 | tf_op jit(solution)/shard_map/convert_element_type | solution.py:178
  383.5 4.3 broadcast.237.clone.1
  387.8 6.3 %scatter_fusion.1 = f32[32,128,512]{2,1,0:T(8,128)} fusion(f32[32,128,512]{2,1,0:T(8,128)} %broadcast.237.clone.1, s32[12]{0:T(128)S(1)} %fusion.22, f32[12,128,512]{2,1,0:T(8,128)S(1)} %reshape.389), kind=kCustom, calls=%fused_computation.3 | custom fusion | bytes 9437232 | tf_op jit(solution)/shard_map/scatter | solution.py:174
  394.1 6.2 %convert_element_type.73 = bf16[32,128,512]{2,1,0:T(8,128)(2,1)} convert(f32[32,128,512]{2,1,0:T(8,128)} %scatter_fusion.1) | non-fusion elementwise | flops 2097152 | bytes 12582912 | tf_op jit(solution)/shard_map/convert_element_type | solution.py:184
  402.6 4.4 all-to-all-start.5
  425.2 4.5 all-to-all-start.4
  431.6 24.0 %reduce-scatter.3.cloned.1.call-done = bf16[128,512]{1,0:T(8,128)(2,1)} async-done(((bf16[4096,512]{1,0:T(8,128)(2,1)}), bf16[128,512]{1,0:T(8,128)(2,1)}) %reduce-scatter.3.cloned.1.call-update) | async-done | bytes 131088 | tf_op jit(solution)/shard_map/reduce_scatter | solution.py:177
  455.6 85.2 %reduce-scatter.5.cloned.1.call-done = bf16[128,512]{1,0:T(8,128)(2,1)} async-done(((bf16[4096,512]{1,0:T(8,128)(2,1)}), bf16[128,512]{1,0:T(8,128)(2,1)}) %reduce-scatter.5.cloned.1.call-update) | async-done | bytes 131088 | tf_op jit(solution)/shard_map/reduce_scatter | solution.py:183
  543.4 4.1 all-to-all-start.6
  548.5 8.5 %all-to-all-done.6 = bf16[4,192,512]{2,1,0:T(8,128)(2,1)S(1)} async-done(((bf16[4,192,512]{2,1,0:T(8,128)(2,1)}), bf16[4,192,512]{2,1,0:T(8,128)(2,1)S(1)}, u32[]{:S(2)}, u32[]{:S(2)}) %all-to-all-start.6) | async-done | bytes 786464 | tf_op jit(solution)/shard_map/all_to_all | solution.py:209
  (426 shorter events, 300.6 us)
Async XLA Ops:
  7.2 8.0 %copy-start.21 = (s32[192,16]{0,1:T(8,128)S(1)}, s32[192,16]{0,1:T(8,128)}, u32[]{:S(2)}) copy-start(s32[192,16]{0,1:T(8,128)} %param.15) | copy-start | bytes 36868
  7.2 20.1 %copy-start.16 = (bf16[192,2048]{1,0:T(8,128)(2,1)S(1)}, bf16[192,2048]{1,0:T(8,128)(2,1)}, u32[]{:S(2)}) copy-start(bf16[192,2048]{1,0:T(8,128)(2,1)} %param.13) | copy-start | bytes 2359300
  9.3 17.2 %all-to-all-start.1 = ((bf16[192,4,512]{2,0,1:T(8,128)(2,1)}), bf16[192,4,512]{2,0,1:T(8,128)(2,1)S(1)}, u32[]{:S(2)}, u32[]{:S(2)}) async-start(bf16[192,4,512]{2,0,1:T(8,128)(2,1)} %bitcast.108), calls=%async_computation.1 | async-start | bytes 1572864 | tf_op jit(solution)/shard_map/all_to_all | solution.py:25
  15.2 25.9 %copy-start.17 = (bf16[192,2048]{1,0:T(8,128)(2,1)S(1)}, bf16[192,2048]{1,0:T(8,128)(2,1)}, u32[]{:S(2)}) copy-start(bf16[192,2048]{1,0:T(8,128)(2,1)} %param.11) | copy-start | bytes 2359300
  15.2 73.8 %all-gather.5.cloned.1.call-start = ((), (), s32[]{:S(2)}) async-start(), calls=%async_computation.12 | async-start | bytes 4325376 | tf_op jit(solution)/shard_map/all_gather | solution.py:52
  27.3 94.9 %all-gather.7.cloned.1.call-start = ((), (), s32[]{:S(2)}) async-start(), calls=%async_computation.13 | async-start | bytes 4325376 | tf_op jit(solution)/shard_map/all_gather | solution.py:55
  27.4 18.2 %copy-start.18 = (bf16[192,2048]{1,0:T(8,128)(2,1)S(1)}, bf16[192,2048]{1,0:T(8,128)(2,1)}, u32[]{:S(2)}) copy-start(bf16[192,2048]{1,0:T(8,128)(2,1)} %param.14) | copy-start | bytes 2359300
  42.1 12.7 %all-to-all-start = ((bf16[192,4,512]{2,0,1:T(8,128)(2,1)}), bf16[192,4,512]{2,0,1:T(8,128)(2,1)S(1)}, u32[]{:S(2)}, u32[]{:S(2)}) async-start(bf16[192,4,512]{2,0,1:T(8,128)(2,1)} %bitcast.109), calls=%async_computation | async-start | bytes 1572864 | tf_op jit(solution)/shard_map/all_to_all | solution.py:24
  54.8 18.2 %all-to-all-start.2 = ((bf16[192,4,512]{2,0,1:T(8,128)(2,1)}), bf16[192,4,512]{2,0,1:T(8,128)(2,1)S(1)}, u32[]{:S(2)}, u32[]{:S(2)}) async-start(bf16[192,4,512]{2,0,1:T(8,128)(2,1)} %bitcast.107), calls=%async_computation.2 | async-start | bytes 1572864 | tf_op jit(solution)/shard_map/all_to_all | solution.py:27
  58.3 397.3 %reduce-scatter.3.cloned.1.call-start = ((), (), s32[]{:S(2)}) async-start(), calls=%async_computation.10 | async-start | bytes 4325376 | tf_op jit(solution)/shard_map/reduce_scatter | solution.py:177
  59.9 14.1 %collective-permute-start = (bf16[384,512]{1,0:T(8,128)(2,1)}, bf16[384,512]{1,0:T(8,128)(2,1)}, u32[]{:S(2)}, u32[]{:S(2)}) collective-permute-start(bf16[384,512]{1,0:T(8,128)(2,1)} %bitcast.2), channel_id=1, source_target_pairs={{0,4},{4,8},{8,12},{12,16},{16,20},{20,24},{24,28},{28,32},{32,36}... | collective-permute-start | bytes 1179656 | tf_op jit(solution)/shard_map/ppermute | solution.py:19
  67.7 10.2 %collective-permute-start.1 = (bf16[384,512]{1,0:T(8,128)(2,1)}, bf16[384,512]{1,0:T(8,128)(2,1)S(1)}, u32[]{:S(2)}, u32[]{:S(2)}) collective-permute-start(bf16[384,512]{1,0:T(8,128)(2,1)} %bitcast.13), channel_id=1, source_target_pairs={{0,4},{4,8},{8,12},{12,16},{16,20},{20,24},{24,28},{28,32},{32,36}... | collective-permute-start | bytes 1179656 | tf_op jit(solution)/shard_map/ppermute | solution.py:19
  75.3 8.0 %copy-start.14 = (bf16[768,4,128]{2,1,0:T(4,128)(2,1)S(1)}, bf16[768,4,128]{2,1,0:T(4,128)(2,1)}, u32[]{:S(2)}) copy-start(bf16[768,4,128]{2,1,0:T(4,128)(2,1)} %concatenate.35) | copy-start | bytes 2359300
  176.1 6.7 %copy-start.7 = (bf16[2048,4,128]{2,0,1:T(8,128)(2,1)}, bf16[2048,4,128]{2,0,1:T(8,128)(2,1)S(1)}, u32[]{:S(2)}) copy-start(bf16[2048,4,128]{2,0,1:T(8,128)(2,1)S(1)} %constant_dynamic-update-slice_fusion.5) | copy-start | bytes 6291460 | tf_op jit(solution)/shard_map/while
  212.7 6.7 %copy-start.7 = (bf16[2048,4,128]{2,0,1:T(8,128)(2,1)}, bf16[2048,4,128]{2,0,1:T(8,128)(2,1)S(1)}, u32[]{:S(2)}) copy-start(bf16[2048,4,128]{2,0,1:T(8,128)(2,1)S(1)} %constant_dynamic-update-slice_fusion.5) | copy-start | bytes 6291460 | tf_op jit(solution)/shard_map/while
  249.4 6.7 %copy-start.7 = (bf16[2048,4,128]{2,0,1:T(8,128)(2,1)}, bf16[2048,4,128]{2,0,1:T(8,128)(2,1)S(1)}, u32[]{:S(2)}) copy-start(bf16[2048,4,128]{2,0,1:T(8,128)(2,1)S(1)} %constant_dynamic-update-slice_fusion.5) | copy-start | bytes 6291460 | tf_op jit(solution)/shard_map/while
  375.5 165.3 %reduce-scatter.5.cloned.1.call-start = ((), (), s32[]{:S(2)}) async-start(), calls=%async_computation.11 | async-start | bytes 4325376 | tf_op jit(solution)/shard_map/reduce_scatter | solution.py:183
  402.6 12.9 %copy-start.22 = (s32[3]{0:T(128)S(1)}, s32[3]{0:T(128)}, u32[]{:S(2)}) copy-start(s32[3]{0:T(128)} %constant.137.clone.1) | copy-start | bytes 40
  402.6 22.6 %all-to-all-start.5 = ((bf16[4,192,512]{2,1,0:T(8,128)(2,1)}), bf16[4,192,512]{2,1,0:T(8,128)(2,1)}, u32[]{:S(2)}, u32[]{:S(2)}) async-start(bf16[4,192,512]{2,1,0:T(8,128)(2,1)} %all_to_all.116), calls=%async_computation.5 | async-start | bytes 1572864 | tf_op jit(solution)/shard_map/all_to_all | solution.py:208
  409.1 20.6 %collective-permute-start.3 = (bf16[384,512]{1,0:T(8,128)(2,1)}, bf16[384,512]{1,0:T(8,128)(2,1)S(1)}, u32[]{:S(2)}, u32[]{:S(2)}) collective-permute-start(bf16[384,512]{1,0:T(8,128)(2,1)} %copy.157), channel_id=1, source_target_pairs={{4,0},{8,4},{12,8},{16,12},{20,16},{24,20},{28,24},{32,28},{36,32}... | collective-permute-start | bytes 1179656 | tf_op jit(solution)/shard_map/ppermute | solution.py:19
  413.6 16.4 %collective-permute-start.2 = (bf16[384,512]{1,0:T(8,128)(2,1)}, bf16[384,512]{1,0:T(8,128)(2,1)}, u32[]{:S(2)}, u32[]{:S(2)}) collective-permute-start(bf16[384,512]{1,0:T(8,128)(2,1)} %copy.155), channel_id=1, source_target_pairs={{4,0},{8,4},{12,8},{16,12},{20,16},{24,20},{28,24},{32,28},{36,32}... | collective-permute-start | bytes 1179656 | tf_op jit(solution)/shard_map/ppermute | solution.py:19
  425.2 118.2 %all-to-all-start.4 = ((bf16[4,192,512]{2,1,0:T(8,128)(2,1)}), bf16[4,192,512]{2,1,0:T(8,128)(2,1)}, u32[]{:S(2)}, u32[]{:S(2)}) async-start(bf16[4,192,512]{2,1,0:T(8,128)(2,1)} %all_to_all.112), calls=%async_computation.4 | async-start | bytes 1572864 | tf_op jit(solution)/shard_map/all_to_all | solution.py:207
  543.4 13.6 %all-to-all-start.6 = ((bf16[4,192,512]{2,1,0:T(8,128)(2,1)}), bf16[4,192,512]{2,1,0:T(8,128)(2,1)S(1)}, u32[]{:S(2)}, u32[]{:S(2)}) async-start(bf16[4,192,512]{2,1,0:T(8,128)(2,1)} %bitcast.175), calls=%async_computation.7 | async-start | bytes 1572864 | tf_op jit(solution)/shard_map/all_to_all | solution.py:209
  557.0 11.8 %all-to-all-start.7 = ((bf16[4,192,512]{2,1,0:T(8,128)(2,1)}), bf16[4,192,512]{2,1,0:T(8,128)(2,1)S(1)}, u32[]{:S(2)}, u32[]{:S(2)}) async-start(bf16[4,192,512]{2,1,0:T(8,128)(2,1)} %bitcast.31), calls=%async_computation.9 | async-start | bytes 1572864 | tf_op jit(solution)/shard_map/all_to_all | solution.py:210
  (74 other events, 260.4 us)
Sparse Core Ops, SparseCore 0:
  27.4 47.0 all-gather.4
  76.7 45.3 all-gather.6
  375.6 79.9 reduce-scatter.2
  459.6 81.1 reduce-scatter.4
where the time goes:
time: 583 us; the launch traced here: 576 us
  local copies, waits for them, and re-layouts  175 us (30%)
  waiting for transfers between devices  166 us (28%)
  other arithmetic  83.8 us (14%)
  matrix products  74.7 us (13%)
  starting transfers between devices  42.7 us (7%)
  between operations  16.1 us (3%)
  blocking collectives  13 us (2%)
    reduce_scatter x1, waiting for transfers between devices, per_device(): lax.psum_scatter(slot_values.reshape(cycle_size * owned_count * BLOCK, fe...  85.2 us
    while x156, local copies, waits for them, and re-layouts  40.2 us
    all_gather x1, waiting for transfers between devices, per_device(): lax.all_gather(offer_values.reshape(owned_count * BLOCK, features), 'ctx'...  25.3 us
    reduce_scatter x1, waiting for transfers between devices, per_device(): lax.psum_scatter(slot_keys.reshape(cycle_size * owned_count * BLOCK, feat...  24 us
    dynamic_update_slice x6, other arithmetic, attend_block(): lax.dynamic_update_slice_in_dim(value_ext, lax.dynamic_slice_in_dim(value...  21.6 us
    sub x6, matrix products, attend_block(): exponent = jnp.exp(masked - row_top)  20.4 us
    dynamic_slice x24, local copies, waits for them, and re-layouts, per_device(): lax.scan(attend_block, (ext_zero, ext_zero, pool_zero, pool_zero), operands)  20.3 us
    convert_element_type x6, other arithmetic, attend_block(): weights = weights_wide.astype(jnp.bfloat16)  16.7 us
  transfers between devices with their start and end apart: 15, of which 8 were waited for; matrix products, arithmetic and copies ran while one was open for 13% of the time, Pallas kernels for 0%

commit v1 on v0

v1 whole, which is shorter than its diff:
```python
import functools
import math

import jax
import jax.numpy as jnp
from jax import lax
from jax.experimental import pallas as pl
from jax.experimental.pallas import tpu as pltpu
from jax.sharding import PartitionSpec as P

D = 128
B = 128
NB = 6
NF = 12
EDGE = 384
T = 768
F32 = jnp.float32
BF = jnp.bfloat16
C2 = math.log2(math.e) / math.sqrt(D)


def nt(a, b):
    return lax.dot_general(a, b, (((1,), (1,)), ((), ())), preferred_element_type=F32)


def tn(a, b):
    return lax.dot_general(a, b, (((0,), (0,)), ((), ())), preferred_element_type=F32)


def nn(a, b):
    return jnp.dot(a, b, preferred_element_type=F32)


def near_span(w):
    return max(0, w - 3) * B, (min(NB - 1, w) + 1) * B


def kern(q_ref, g_ref, kw_ref, vw_ref, kp_ref, vp_ref, fb_ref, nb_ref,
         o_ref, dq_ref, dkw_ref, dvw_ref, dkp_ref, dvp_ref,
         sf, sn, ef, en, m_s, l_s, ot_s, dqt_s):
    q = q_ref[...]
    g = g_ref[...]
    qt = q.T
    tri = lax.broadcasted_iota(jnp.int32, (B, B), 0) <= lax.broadcasted_iota(jnp.int32, (B, B), 1)
    m_s[...] = jnp.full((1, T), -jnp.inf, F32)
    for i in range(NF):
        s = nn(kp_ref[i * B:(i + 1) * B, :], qt)
        sf[i] = s
        m_s[...] = jnp.maximum(m_s[...], jnp.max(s, axis=0, keepdims=True) - fb_ref[i:i + 1, :])
    for w in range(NB + 3):
        lo, hi = near_span(w)
        s = nn(kw_ref[w * B:(w + 1) * B, :], qt[:, lo:hi])
        if w >= 3:
            s = jnp.concatenate([jnp.where(tri, s[:, :B], -jnp.inf), s[:, B:]], 1) if hi - lo > B else jnp.where(tri, s, -jnp.inf)
        sn[w, :, :hi - lo] = s
        m_s[:, lo:hi] = jnp.maximum(m_s[:, lo:hi], jnp.max(s, axis=0, keepdims=True) - nb_ref[w:w + 1, lo:hi])
    m = m_s[...]
    l_s[...] = jnp.zeros((1, T), F32)
    ot_s[...] = jnp.zeros((D, T), F32)
    for i in range(NF):
        e = jnp.exp2((sf[i] - (m + fb_ref[i:i + 1, :])) * C2)
        l_s[...] += jnp.sum(e, axis=0, keepdims=True)
        e = e.astype(BF)
        ef[i] = e
        ot_s[...] += tn(vp_ref[i * B:(i + 1) * B, :], e)
    for w in range(NB + 3):
        lo, hi = near_span(w)
        e = jnp.exp2((sn[w, :, :hi - lo] - (m[:, lo:hi] + nb_ref[w:w + 1, lo:hi])) * C2)
        l_s[:, lo:hi] += jnp.sum(e, axis=0, keepdims=True)
        e = e.astype(BF)
        en[w, :, :hi - lo] = e
        ot_s[:, lo:hi] += tn(vw_ref[w * B:(w + 1) * B, :], e)
    inv = 1.0 / l_s[...]
    ot = ot_s[...] * inv
    o_ref[...] = ot.T.astype(BF)
    gt = (g.T.astype(F32) * inv).astype(BF)
    gs = gt.T
    delta = jnp.sum(gt.astype(F32) * ot, axis=0, keepdims=True)
    dqt_s[...] = jnp.zeros((D, T), F32)
    scale = 1.0 / math.sqrt(D)
    for i in range(NF):
        e = ef[i]
        dvp_ref[i * B:(i + 1) * B, :] = nn(e, gs).astype(BF)
        dp = nn(vp_ref[i * B:(i + 1) * B, :], gt)
        ds = (e.astype(F32) * (dp - delta)).astype(BF)
        dkp_ref[i * B:(i + 1) * B, :] = (nn(ds, q) * scale).astype(BF)
        dqt_s[...] += tn(kp_ref[i * B:(i + 1) * B, :], ds)
    for w in range(NB + 3):
        lo, hi = near_span(w)
        e = en[w, :, :hi - lo]
        dvw_ref[w * B:(w + 1) * B, :] = nn(e, gs[lo:hi])
        dp = nn(vw_ref[w * B:(w + 1) * B, :], gt[:, lo:hi])
        ds = (e.astype(F32) * (dp - delta[:, lo:hi])).astype(BF)
        dkw_ref[w * B:(w + 1) * B, :] = nn(ds, q[lo:hi]) * scale
        dqt_s[:, lo:hi] += tn(kw_ref[w * B:(w + 1) * B, :], ds)
    dq_ref[...] = (dqt_s[...].T * scale).astype(BF)


def attend(q, g, kw, vw, kp, vp, fb, nb):
    def col(rows):
        return pl.BlockSpec((rows, D), lambda h: (0, h))
    full = lambda a: pl.BlockSpec(a.shape, lambda h: (0, 0))
    H = q.shape[1] // D
    W = (NB + 3) * B
    return pl.pallas_call(
        kern,
        grid=(H,),
        in_specs=[col(T), col(T), col(W), col(W), col(NF * B), col(NF * B), full(fb), full(nb)],
        out_specs=[col(T), col(T), col(W), col(W), col(NF * B), col(NF * B)],
        out_shape=[jax.ShapeDtypeStruct((T, H * D), BF)] * 2
        + [jax.ShapeDtypeStruct((W, H * D), F32)] * 2
        + [jax.ShapeDtypeStruct((NF * B, H * D), BF)] * 2,
        scratch_shapes=[
            pltpu.VMEM((NF, B, T), F32),
            pltpu.VMEM((NB + 3, B, 512), F32),
            pltpu.VMEM((NF, B, T), BF),
            pltpu.VMEM((NB + 3, B, 512), BF),
            pltpu.VMEM((1, T), F32),
            pltpu.VMEM((1, T), F32),
            pltpu.VMEM((D, T), F32),
            pltpu.VMEM((D, T), F32),
        ],
        compiler_params=pltpu.CompilerParams(vmem_limit_bytes=48 * 1024 * 1024),
    )(q, g, kw, vw, kp, vp, fb, nb)


def shifted(value, steps):
    count = lax.axis_size("ctx")
    first, last = (max(0, -steps), min(count, count - steps))
    return lax.ppermute(value, "ctx", [(s, s + steps) for s in range(first, last)])


ROW = 8
ROWS = 4
ROW_GROUPS = [[r * ROW + i for i in range(ROW)] for r in range(ROWS)]
COL_GROUPS = [[r * ROW + i for r in range(ROWS)] for i in range(ROW)]


def biases(pattern, phase, device):
    rows = lax.dynamic_slice_in_dim(pattern, device * NB, NB, 0)
    ids = phase + 16 * jnp.arange(NF, dtype=jnp.int32)
    far = jnp.any(rows[None, :, 4:] == ids[:, None, None], axis=2)
    fb = jnp.where(far, 0.0, jnp.inf).astype(F32)
    blocks = device * NB - 3 + jnp.arange(NB + 3, dtype=jnp.int32)
    nb = jnp.where(blocks >= 0, 0.0, jnp.inf).astype(F32)
    return jnp.repeat(fb, B, axis=1), jnp.broadcast_to(nb[:, None], (NB + 3, T))


def per_device(queries, keys, values, grad_out, pattern):
    a2a = functools.partial(lax.all_to_all, axis_name="head", split_axis=1, concat_axis=0, tiled=True)
    k, v, q, g = a2a(keys), a2a(values), a2a(queries), a2a(grad_out)
    device = lax.axis_index("ctx")
    phase = pattern[pattern.shape[0] - 1, 4] % 16
    own = jnp.mod(phase - device * NB, 16)
    valid = own < NB
    own = jnp.where(valid, own, 0) * B
    slot = jnp.where(
        valid,
        jnp.concatenate([lax.dynamic_slice_in_dim(k, own, B, 0), lax.dynamic_slice_in_dim(v, own, B, 0)], 0),
        0,
    )
    row = lax.all_gather(slot, "ctx", axis=0, tiled=True, axis_index_groups=ROW_GROUPS)
    places = [(phase + 16 * j) // NB * (2 * B) for j in range(3)]
    three = jnp.concatenate([lax.dynamic_slice_in_dim(row, p, 2 * B, 0) for p in places], 0)
    pool = lax.all_gather(three, "ctx", axis=0, tiled=True, axis_index_groups=COL_GROUPS)
    pool = pool.reshape(NF, 2, B, 512)
    kp, vp = pool[:, 0].reshape(NF * B, 512), pool[:, 1].reshape(NF * B, 512)
    before_k, before_v = shifted((k[T - EDGE:], v[T - EDGE:]), 1)
    kw, vw = jnp.concatenate([before_k, k], 0), jnp.concatenate([before_v, v], 0)
    fb, nb = biases(pattern, phase, device)
    o, dq, dkw, dvw, dkp, dvp = attend(q, g, kw, vw, kp, vp, fb, nb)
    back_k, back_v = shifted((dkw[:EDGE].astype(BF), dvw[:EDGE].astype(BF)), -1)
    both = jnp.stack([dkp.reshape(NF, B, 512), dvp.reshape(NF, B, 512)], 1).reshape(NF * 2 * B, 512)
    mine3 = lax.psum_scatter(both, "ctx", scatter_dimension=0, tiled=True, axis_index_groups=COL_GROUPS)
    slots = jnp.zeros((ROW * 2 * B, 512), BF)
    for j in range(3):
        slots = lax.dynamic_update_slice_in_dim(slots, mine3[j * 2 * B:(j + 1) * 2 * B], places[j], 0)
    mine = lax.psum_scatter(slots, "ctx", scatter_dimension=0, tiled=True, axis_index_groups=ROW_GROUPS)
    mine = jnp.where(valid, mine.astype(F32), 0.0)

    def merged(ext, back, extra):
        total = ext[EDGE:] + jnp.pad(back.astype(F32), ((T - EDGE, 0), (0, 0)))
        total = lax.dynamic_update_slice_in_dim(
            total, lax.dynamic_slice_in_dim(total, own, B, 0) + extra, own, 0
        )
        return total.astype(BF)

    dk = merged(dkw, back_k, mine[:B])
    dv = merged(dvw, back_v, mine[B:])
    out = functools.partial(lax.all_to_all, axis_name="head", split_axis=0, concat_axis=1, tiled=True)
    return out(o), out(dq), out(dk), out(dv)


def solution(mesh):
    split = P(("ctx", "head"), None)
    return jax.shard_map(
        per_device, mesh=mesh, in_specs=(split,) * 4 + (P(),), out_specs=(split,) * 4, check_vma=False
    )
```

time: 583 us -> 279 us (0.48)
  local copies, waits for them, and re-layouts: 175 us -> 23.5 us
  matrix products: 74.7 us -> 0 us
  other arithmetic: 83.8 us -> 13.7 us
  Pallas kernels: 0 us -> 35.7 us
  waiting for transfers between devices: 166 us -> 142 us
  blocking collectives: 13 us -> 0 us
    reduce_scatter x2, waiting for transfers between devices: 109 us -> 52.9 us  [the longest x1 44.8 us: per_device(): lax.psum_scatter(both, 'ctx', scatter_dimension=0, tiled=True, axis_index...]
    dot_general x30 -> x0, matrix products: 54.3 us -> none  [the longest x6 15.5 us: attend_block(): jnp.einsum('qhd,khd->hqk', grad_block, joined_values, preferred_element_t...]
    while x158 -> x0, local copies, waits for them, and re-layouts: 46.2 us -> none
    pallas_call x0 -> x1, Pallas kernels: none -> 35.7 us  [attend(): pl.pallas_call(kern, grid=(H,), in_specs=[col(T), col(T), col(W), col(W),...]
    convert_element_type x10 -> x2, other arithmetic: 30.8 us -> 1.97 us  [merged(): return total.astype(BF)]
    dynamic_slice x37 -> x3, local copies, waits for them, and re-layouts: 28.8 us -> 1.18 us  [the longest x1 1.16 us: per_device(): lax.dynamic_slice_in_dim(row, p, 2 * B, 0)]
    dynamic_update_slice x6 -> x1, other arithmetic: 21.6 us -> 0.13 us  [merged(): lax.dynamic_update_slice_in_dim(total, lax.dynamic_slice_in_dim(total, ow...]
    sub x6 -> x0, matrix products: 20.4 us -> none  [attend_block(): exponent = jnp.exp(masked - row_top)]
  transfers between devices with their start and end apart: 15 -> 16, of which waited for: 8 -> 11; matrix products, arithmetic and copies ran while one was open for 13% -> 9% of each run, Pallas kernels for 0% -> 0%
where the time goes in v1:
time: 279 us; the launch traced here: 274 us
  waiting for transfers between devices  142 us (51%)
  starting transfers between devices  42.9 us (15%)
  Pallas kernels  35.7 us (13%)
  local copies, waits for them, and re-layouts  23.5 us (8%)
  between operations  16.1 us (6%)
  other arithmetic  13.7 us (5%)
    reduce_scatter x1, waiting for transfers between devices, per_device(): lax.psum_scatter(both, 'ctx', scatter_dimension=0, tiled=True, axis_index...  44.8 us
    pallas_call x1, Pallas kernels, attend(): pl.pallas_call(kern, grid=(H,), in_specs=[col(T), col(T), col(W), col(W),...  35.7 us
    all_gather x1, waiting for transfers between devices, per_device(): lax.all_gather(slot, 'ctx', axis=0, tiled=True, axis_index_groups=ROW_GRO...  27.6 us
    all_to_all x4, waiting for transfers between devices, per_device(): return (out(o), out(dq), out(dk), out(dv))  23.6 us
    all_to_all x4, waiting for transfers between devices, per_device(): k, v, q, g = (a2a(keys), a2a(values), a2a(queries), a2a(grad_out))  21.5 us
    all_to_all x4, starting transfers between devices, per_device(): k, v, q, g = (a2a(keys), a2a(values), a2a(queries), a2a(grad_out))  17.7 us
    all_gather x1, waiting for transfers between devices, per_device(): lax.all_gather(three, 'ctx', axis=0, tiled=True, axis_index_groups=COL_GR...  16.5 us
    all_to_all x4, starting transfers between devices, per_device(): return (out(o), out(dq), out(dk), out(dv))  16.1 us
  transfers between devices with their start and end apart: 16, of which 11 were waited for; matrix products, arithmetic and copies ran while one was open for 9% of the time, Pallas kernels for 0%

profile of v1, /device:TPU:1, one launch (start us, length us, event | category | flops | bytes accessed | tf_op | source)
XLA Modules:
  0.0 274.0 jit_solution(15205117053552451144)
XLA Ops:
  7.2 2.2 copy.51
  9.3 5.9 %all-to-all-start.2 = ((bf16[192,4,512]{2,0,1:T(8,128)(2,1)}), bf16[192,4,512]{2,0,1:T(8,128)(2,1)S(1)}, u32[]{:S(2)}, u32[]{:S(2)}) async-start(bf16[192,4,512]{2,0,1:T(8,128)(2,1)} %bitcast.61), calls=%async_computation.2 | async-start | bytes 1572864 | tf_op jit(solution)/shard_map/all_to_all | solution.py:151
  16.1 10.4 %all-to-all-done.2 = bf16[192,4,512]{2,0,1:T(8,128)(2,1)S(1)} async-done(((bf16[192,4,512]{2,0,1:T(8,128)(2,1)}), bf16[192,4,512]{2,0,1:T(8,128)(2,1)S(1)}, u32[]{:S(2)}, u32[]{:S(2)}) %all-to-all-start.2) | async-done | bytes 786464 | tf_op jit(solution)/shard_map/all_to_all | solution.py:151
  26.6 3.5 %all-to-all-start.3 = ((bf16[192,4,512]{2,0,1:T(8,128)(2,1)}), bf16[192,4,512]{2,0,1:T(8,128)(2,1)S(1)}, u32[]{:S(2)}, u32[]{:S(2)}) async-start(bf16[192,4,512]{2,0,1:T(8,128)(2,1)} %bitcast.60), calls=%async_computation.3 | async-start | bytes 1572864 | tf_op jit(solution)/shard_map/all_to_all | solution.py:151
  32.7 7.5 %all-to-all-done.3 = bf16[192,4,512]{2,0,1:T(8,128)(2,1)S(1)} async-done(((bf16[192,4,512]{2,0,1:T(8,128)(2,1)}), bf16[192,4,512]{2,0,1:T(8,128)(2,1)S(1)}, u32[]{:S(2)}, u32[]{:S(2)}) %all-to-all-start.3) | async-done | bytes 786464 | tf_op jit(solution)/shard_map/all_to_all | solution.py:151
  41.2 27.6 %all-gather.3.cloned.1.call-done = bf16[2048,512]{1,0:T(8,128)(2,1)} async-done(((bf16[256,512]{1,0:T(8,128)(2,1)}), bf16[2048,512]{1,0:T(8,128)(2,1)}) %all-gather.3.cloned.1.call-update) | async-done | bytes 2097168 | tf_op jit(solution)/shard_map/all_gather | solution.py:162
  72.3 4.1 %all-to-all-start = ((bf16[192,4,512]{2,0,1:T(8,128)(2,1)}), bf16[192,4,512]{2,0,1:T(8,128)(2,1)S(1)}, u32[]{:S(2)}, u32[]{:S(2)}) async-start(bf16[192,4,512]{2,0,1:T(8,128)(2,1)} %bitcast.77), calls=%async_computation | async-start | bytes 1572864 | tf_op jit(solution)/shard_map/all_to_all | solution.py:151
  76.6 2.6 collective-permute-start
  84.6 3.6 %all-to-all-done = bf16[192,4,512]{2,0,1:T(8,128)(2,1)S(1)} async-done(((bf16[192,4,512]{2,0,1:T(8,128)(2,1)}), bf16[192,4,512]{2,0,1:T(8,128)(2,1)S(1)}, u32[]{:S(2)}, u32[]{:S(2)}) %all-to-all-start) | async-done | bytes 786464 | tf_op jit(solution)/shard_map/all_to_all | solution.py:151
  88.3 4.2 %all-to-all-start.1 = ((bf16[192,4,512]{2,0,1:T(8,128)(2,1)}), bf16[192,4,512]{2,0,1:T(8,128)(2,1)}, u32[]{:S(2)}, u32[]{:S(2)}) async-start(bf16[192,4,512]{2,0,1:T(8,128)(2,1)} %bitcast.78), calls=%async_computation.1 | async-start | bytes 1572864 | tf_op jit(solution)/shard_map/all_to_all | solution.py:151
  93.8 16.5 %all-gather.5.cloned.1.call-done = bf16[3072,512]{1,0:T(8,128)(2,1)} async-done(((bf16[768,512]{1,0:T(8,128)(2,1)}), bf16[3072,512]{1,0:T(8,128)(2,1)}) %all-gather.5.cloned.1.call-update) | async-done | bytes 3145744 | tf_op jit(solution)/shard_map/all_gather | solution.py:165
  110.3 3.9 %fusion.2 = (bf16[12,1,128,512]{3,2,1,0:T(8,128)(2,1)}, bf16[12,1,128,512]{3,2,1,0:T(8,128)(2,1)}) fusion(bf16[12,2,128,512]{3,2,1,0:T(8,128)(2,1)} %bitcast.75), kind=kLoop, calls=%fused_computation.30 | loop fusion | bytes 6291456 | tf_op jit(solution)/shard_map/slice | solution.py:167
  114.3 35.7 %shard_map.84 = (bf16[768,512]{1,0:T(8,128)(2,1)}, bf16[768,512]{1,0:T(8,128)(2,1)}, f32[1152,512]{1,0:T(8,128)}, f32[1152,512]{1,0:T(8,128)}, bf16[1536,512]{1,0:T(8,128)(2,1)}, /*index=5*/bf16[1536,512]{1,0:T(8,128)(2,1)}) custom-call(bf16[768,512]{1,0:T(8,128)(2,1)S(1)} %bitcast.64, bf16[768,512]{1,0:T(8,128)(2,1)} %bitcast.3.g_ref, ...), custom_call_target="tpu_custom_call" | custom-call | tf_op jit(solution)/shard_map/pallas_call | solution.py:105
  150.0 3.8 %pad_maximum_fusion = bf16[12,2,128,512]{3,2,1,0:T(8,128)(2,1)} fusion(bf16[12,1,128,512]{3,2,1,0:T(8,128)(2,1)} %bitcast.84, bf16[12,1,128,512]{3,2,1,0:T(8,128)(2,1)} %bitcast.83), kind=kLoop, calls=%fused_computation | loop fusion | flops 1572864 | bytes 6291456 | tf_op jit(solution)/shard_map/stack | solution.py:173
  153.9 44.8 %reduce-scatter.3.cloned.1.call-done = bf16[768,512]{1,0:T(8,128)(2,1)} async-done(((bf16[3072,512]{1,0:T(8,128)(2,1)}), bf16[768,512]{1,0:T(8,128)(2,1)}) %reduce-scatter.3.cloned.1.call-update) | async-done | bytes 786448 | tf_op jit(solution)/shard_map/reduce_scatter | solution.py:174
  202.5 2.5 collective-permute-start.2
  205.1 4.2 %all-to-all-start.4 = ((bf16[4,192,512]{2,1,0:T(8,128)(2,1)}), bf16[4,192,512]{2,1,0:T(8,128)(2,1)S(1)}, u32[]{:S(2)}, u32[]{:S(2)}) async-start(bf16[4,192,512]{2,1,0:T(8,128)(2,1)} %bitcast.16), calls=%async_computation.4 | async-start | bytes 1572864 | tf_op jit(solution)/shard_map/all_to_all | solution.py:191
  214.0 7.9 %all-to-all-done.4 = bf16[4,192,512]{2,1,0:T(8,128)(2,1)S(1)} async-done(((bf16[4,192,512]{2,1,0:T(8,128)(2,1)}), bf16[4,192,512]{2,1,0:T(8,128)(2,1)S(1)}, u32[]{:S(2)}, u32[]{:S(2)}) %all-to-all-start.4) | async-done | bytes 786464 | tf_op jit(solution)/shard_map/all_to_all | solution.py:191
  221.9 4.2 %all-to-all-start.5 = ((bf16[4,192,512]{2,1,0:T(8,128)(2,1)}), bf16[4,192,512]{2,1,0:T(8,128)(2,1)}, u32[]{:S(2)}, u32[]{:S(2)}) async-start(bf16[4,192,512]{2,1,0:T(8,128)(2,1)} %bitcast.18), calls=%async_computation.5 | async-start | bytes 1572864 | tf_op jit(solution)/shard_map/all_to_all | solution.py:191
  227.8 8.1 %reduce-scatter.5.cloned.1.call-done = bf16[256,512]{1,0:T(8,128)(2,1)} async-done(((bf16[2048,512]{1,0:T(8,128)(2,1)}), bf16[256,512]{1,0:T(8,128)(2,1)}) %reduce-scatter.5.cloned.1.call-update) | async-done | bytes 262160 | tf_op jit(solution)/shard_map/reduce_scatter | solution.py:178
  238.1 4.2 %all-to-all-start.6 = ((bf16[4,192,512]{2,1,0:T(8,128)(2,1)}), bf16[4,192,512]{2,1,0:T(8,128)(2,1)S(1)}, u32[]{:S(2)}, u32[]{:S(2)}) async-start(bf16[4,192,512]{2,1,0:T(8,128)(2,1)} %bitcast.82), calls=%async_computation.8 | async-start | bytes 1572864 | tf_op jit(solution)/shard_map/all_to_all | solution.py:191
  243.3 10.0 %all-to-all-done.6 = bf16[4,192,512]{2,1,0:T(8,128)(2,1)S(1)} async-done(((bf16[4,192,512]{2,1,0:T(8,128)(2,1)}), bf16[4,192,512]{2,1,0:T(8,128)(2,1)S(1)}, u32[]{:S(2)}, u32[]{:S(2)}) %all-to-all-start.6) | async-done | bytes 786464 | tf_op jit(solution)/shard_map/all_to_all | solution.py:191
  253.3 3.5 %all-to-all-start.7 = ((bf16[4,192,512]{2,1,0:T(8,128)(2,1)}), bf16[4,192,512]{2,1,0:T(8,128)(2,1)S(1)}, u32[]{:S(2)}, u32[]{:S(2)}) async-start(bf16[4,192,512]{2,1,0:T(8,128)(2,1)} %bitcast.81), calls=%async_computation.9 | async-start | bytes 1572864 | tf_op jit(solution)/shard_map/all_to_all | solution.py:191
  260.8 5.6 %all-to-all-done.7 = bf16[4,192,512]{2,1,0:T(8,128)(2,1)S(1)} async-done(((bf16[4,192,512]{2,1,0:T(8,128)(2,1)}), bf16[4,192,512]{2,1,0:T(8,128)(2,1)S(1)}, u32[]{:S(2)}, u32[]{:S(2)}) %all-to-all-start.7) | async-done | bytes 786464 | tf_op jit(solution)/shard_map/all_to_all | solution.py:191
  (71 shorter events, 31.5 us)
Async XLA Ops:
  7.2 8.0 %copy-start.4 = (bf16[192,2048]{1,0:T(8,128)(2,1)S(1)}, bf16[192,2048]{1,0:T(8,128)(2,1)}, u32[]{:S(2)}) copy-start(bf16[192,2048]{1,0:T(8,128)(2,1)} %param.7) | copy-start | bytes 2359300
  9.3 17.2 %all-to-all-start.2 = ((bf16[192,4,512]{2,0,1:T(8,128)(2,1)}), bf16[192,4,512]{2,0,1:T(8,128)(2,1)S(1)}, u32[]{:S(2)}, u32[]{:S(2)}) async-start(bf16[192,4,512]{2,0,1:T(8,128)(2,1)} %bitcast.61), calls=%async_computation.2 | async-start | bytes 1572864 | tf_op jit(solution)/shard_map/all_to_all | solution.py:151
  15.2 14.9 %copy-start.7 = (s32[192,16]{0,1:T(8,128)S(1)}, s32[192,16]{0,1:T(8,128)}, u32[]{:S(2)}) copy-start(s32[192,16]{0,1:T(8,128)} %param.9) | copy-start | bytes 36868
  26.6 13.6 %all-to-all-start.3 = ((bf16[192,4,512]{2,0,1:T(8,128)(2,1)}), bf16[192,4,512]{2,0,1:T(8,128)(2,1)S(1)}, u32[]{:S(2)}, u32[]{:S(2)}) async-start(bf16[192,4,512]{2,0,1:T(8,128)(2,1)} %bitcast.60), calls=%async_computation.3 | async-start | bytes 1572864 | tf_op jit(solution)/shard_map/all_to_all | solution.py:151
  30.1 38.7 %all-gather.3.cloned.1.call-start = ((), (), s32[]{:S(2)}) async-start(), calls=%async_computation.10 | async-start | bytes 2359296 | tf_op jit(solution)/shard_map/all_gather | solution.py:162
  40.2 39.4 %copy-start.1 = (bf16[192,4,512]{2,0,1:T(8,128)(2,1)}, bf16[192,4,512]{2,0,1:T(8,128)(2,1)S(1)}, u32[]{:S(2)}) copy-start(bf16[192,4,512]{2,0,1:T(8,128)(2,1)S(1)} %all-to-all-done.3) | copy-start | bytes 2359300
  41.1 69.3 %all-gather.5.cloned.1.call-start = ((), (), s32[]{:S(2)}) async-start(), calls=%async_computation.11 | async-start | bytes 3932160 | tf_op jit(solution)/shard_map/all_gather | solution.py:165
  69.9 1.4 copy-start.5
  72.3 16.0 %all-to-all-start = ((bf16[192,4,512]{2,0,1:T(8,128)(2,1)}), bf16[192,4,512]{2,0,1:T(8,128)(2,1)S(1)}, u32[]{:S(2)}, u32[]{:S(2)}) async-start(bf16[192,4,512]{2,0,1:T(8,128)(2,1)} %bitcast.77), calls=%async_computation | async-start | bytes 1572864 | tf_op jit(solution)/shard_map/all_to_all | solution.py:151
  76.6 7.9 %collective-permute-start = (bf16[384,512]{1,0:T(8,128)(2,1)S(1)}, bf16[384,512]{1,0:T(8,128)(2,1)S(1)}, u32[]{:S(2)}, u32[]{:S(2)}) collective-permute-start(bf16[384,512]{1,0:T(8,128)(2,1)S(1)} %bitcast.93), channel_id=1, source_target_pairs={{0,4},{4,8},{8,12},{12,16},{16,20},{20,24},{24,28},{28,32},{32,36}... | collective-permute-start | bytes 1179656 | tf_op jit(solution)/shard_map/ppermute | solution.py:130
  80.4 12.2 %collective-permute-start.1 = (bf16[384,512]{1,0:T(8,128)(2,1)}, bf16[384,512]{1,0:T(8,128)(2,1)}, u32[]{:S(2)}, u32[]{:S(2)}) collective-permute-start(bf16[384,512]{1,0:T(8,128)(2,1)} %bitcast.8), channel_id=1, source_target_pairs={{0,4},{4,8},{8,12},{12,16},{16,20},{20,24},{24,28},{28,32},{32,36}... | collective-permute-start | bytes 1179656 | tf_op jit(solution)/shard_map/ppermute | solution.py:130
  88.3 26.0 %all-to-all-start.1 = ((bf16[192,4,512]{2,0,1:T(8,128)(2,1)}), bf16[192,4,512]{2,0,1:T(8,128)(2,1)}, u32[]{:S(2)}, u32[]{:S(2)}) async-start(bf16[192,4,512]{2,0,1:T(8,128)(2,1)} %bitcast.78), calls=%async_computation.1 | async-start | bytes 1572864 | tf_op jit(solution)/shard_map/all_to_all | solution.py:151
  92.5 106.3 %reduce-scatter.3.cloned.1.call-start = ((), (), s32[]{:S(2)}) async-start(), calls=%async_computation.12 | async-start | bytes 3932160 | tf_op jit(solution)/shard_map/reduce_scatter | solution.py:174
  153.9 82.0 %reduce-scatter.5.cloned.1.call-start = ((), (), s32[]{:S(2)}) async-start(), calls=%async_computation.13 | async-start | bytes 2359296 | tf_op jit(solution)/shard_map/reduce_scatter | solution.py:178
  198.7 1.1 copy-start.6
  199.9 1.4 copy-start
  202.5 9.9 %collective-permute-start.2 = (bf16[384,512]{1,0:T(8,128)(2,1)S(1)}, bf16[384,512]{1,0:T(8,128)(2,1)S(1)}, u32[]{:S(2)}, u32[]{:S(2)}) collective-permute-start(bf16[384,512]{1,0:T(8,128)(2,1)S(1)} %slice.95), channel_id=1, source_target_pairs={{4,0},{8,4},{12,8},{16,12},{20,16},{24,20},{28,24},{32,28},{36,32}... | collective-permute-start | bytes 1179656 | tf_op jit(solution)/shard_map/ppermute | solution.py:130
  205.1 16.9 %all-to-all-start.4 = ((bf16[4,192,512]{2,1,0:T(8,128)(2,1)}), bf16[4,192,512]{2,1,0:T(8,128)(2,1)S(1)}, u32[]{:S(2)}, u32[]{:S(2)}) async-start(bf16[4,192,512]{2,1,0:T(8,128)(2,1)} %bitcast.16), calls=%async_computation.4 | async-start | bytes 1572864 | tf_op jit(solution)/shard_map/all_to_all | solution.py:191
  210.5 15.7 %collective-permute-start.3 = (bf16[384,512]{1,0:T(8,128)(2,1)S(1)}, bf16[384,512]{1,0:T(8,128)(2,1)S(1)}, u32[]{:S(2)}, u32[]{:S(2)}) collective-permute-start(bf16[384,512]{1,0:T(8,128)(2,1)S(1)} %slice.94), channel_id=1, source_target_pairs={{4,0},{8,4},{12,8},{16,12},{20,16},{24,20},{28,24},{32,28},{36,32}... | collective-permute-start | bytes 1179656 | tf_op jit(solution)/shard_map/ppermute | solution.py:130
  221.9 4.2 %copy-start.2 = (bf16[4,192,512]{2,1,0:T(8,128)(2,1)}, bf16[4,192,512]{2,1,0:T(8,128)(2,1)S(1)}, u32[]{:S(2)}) copy-start(bf16[4,192,512]{2,1,0:T(8,128)(2,1)S(1)} %all-to-all-done.4) | copy-start | bytes 2359300
  221.9 16.2 %all-to-all-start.5 = ((bf16[4,192,512]{2,1,0:T(8,128)(2,1)}), bf16[4,192,512]{2,1,0:T(8,128)(2,1)}, u32[]{:S(2)}, u32[]{:S(2)}) async-start(bf16[4,192,512]{2,1,0:T(8,128)(2,1)} %bitcast.18), calls=%async_computation.5 | async-start | bytes 1572864 | tf_op jit(solution)/shard_map/all_to_all | solution.py:191
  238.1 15.2 %all-to-all-start.6 = ((bf16[4,192,512]{2,1,0:T(8,128)(2,1)}), bf16[4,192,512]{2,1,0:T(8,128)(2,1)S(1)}, u32[]{:S(2)}, u32[]{:S(2)}) async-start(bf16[4,192,512]{2,1,0:T(8,128)(2,1)} %bitcast.82), calls=%async_computation.8 | async-start | bytes 1572864 | tf_op jit(solution)/shard_map/all_to_all | solution.py:191
  242.3 14.5 %copy-start.3 = (bf16[4,192,512]{2,1,0:T(8,128)(2,1)S(1)}, bf16[4,192,512]{2,1,0:T(8,128)(2,1)}, u32[]{:S(2)}) copy-start(bf16[4,192,512]{2,1,0:T(8,128)(2,1)} %copy-done.2) | copy-start | bytes 2359300
  253.3 13.2 %all-to-all-start.7 = ((bf16[4,192,512]{2,1,0:T(8,128)(2,1)}), bf16[4,192,512]{2,1,0:T(8,128)(2,1)S(1)}, u32[]{:S(2)}, u32[]{:S(2)}) async-start(bf16[4,192,512]{2,1,0:T(8,128)(2,1)} %bitcast.81), calls=%async_computation.9 | async-start | bytes 1572864 | tf_op jit(solution)/shard_map/all_to_all | solution.py:191
Sparse Core Ops, SparseCore 0:
  41.2 27.4 all-gather.2
  71.0 39.3 all-gather.4
  154.0 44.6 reduce-scatter.2
  201.4 34.3 reduce-scatter.4

commit v2 on v1

v2 whole, which is shorter than its diff:
```python
import functools
import math

import jax
import jax.numpy as jnp
from jax import lax
from jax.experimental import pallas as pl
from jax.experimental.pallas import tpu as pltpu
from jax.sharding import PartitionSpec as P

D = 128
B = 128
NB = 6
NF = 12
NW = 9
EDGE = 384
T = 768
W = 1152
R = 192
H = 4
Z = 4
F32 = jnp.float32
BF = jnp.bfloat16
SCALE = 1.0 / math.sqrt(D)
C2 = math.log2(math.e) / math.sqrt(D)
MESH = pl.DeviceIdType.MESH


def tn(a, b):
    return lax.dot_general(a, b, (((0,), (0,)), ((), ())), preferred_element_type=F32)


def nn(a, b):
    return jnp.dot(a, b, preferred_element_type=F32)


def near_span(w):
    return max(0, w - 3) * B, (min(NB - 1, w) + 1) * B


def kernel(
    k_in, v_in, q_in, g_in, pat,
    o_out, dq_out, dk_out, dv_out,
    kb, vb, qb, gb, slot, rows, pool,
    ob, dqb, dkw, dvw, dkb, dvb, back_s, back_r,
    dpool, sib_r, pair, x_r, ysl, y_r, zs, z_r, zown,
    fb, sf, sn, ef, en, m_s, l_s, ot_s, dqt_s, gt_s, gs_s, de_s, qt_s,
    a_s, a_r, h_s, h_r, s1_s, s1_r, y1_s, y1_r, x1_s, x1_r, s2_s, s2_r,
    o_s, o_r, gs_sd, gs_rc, gx_s, gx_rc, gy_s, gy_rc, gz_s, gz_rc, b_s, b_r,
):
    ctx = lax.axis_index("ctx")
    z = lax.axis_index("head")
    c = ctx % 2
    y = (ctx // 2) % 4
    x = ctx // 8
    sib = ctx + 1 - 2 * c
    up = (ctx + 1) % 32
    down = (ctx + 31) % 32

    def xpeer(d):
        return ((x + d) % 4) * 8 + y * 2 + c

    def ypeer(d):
        return x * 8 + ((y + d) % 4) * 2 + c

    def at(ctx_, z_):
        return {"ctx": ctx_, "head": z_}

    def remote(src, dst, ss, rs, dev):
        return pltpu.make_async_remote_copy(
            src_ref=src, dst_ref=dst, send_sem=ss, recv_sem=rs, device_id=dev, device_id_type=MESH
        )

    def done(ref, sem):
        pltpu.make_async_copy(ref, ref, sem).wait()

    barrier = pltpu.get_barrier_semaphore()
    peers = [at(ctx, (z + d) % Z) for d in (1, 2, 3)]
    peers += [at(ypeer(d), z) for d in (1, 2, 3)] + [at(xpeer(d), z) for d in (1, 2, 3)]
    peers += [at(sib, z), at(up, z), at(down, z)]
    for dev in peers:
        pl.semaphore_signal(barrier, inc=1, device_id=dev, device_id_type=MESH)

    phase = pat[NB * 32 - 1, 4] % 16
    own = (phase - ctx * NB + 192) % 16
    ids = phase + 16 * lax.broadcasted_iota(jnp.int32, (16, B), 0)
    for b in range(NB):
        hit = jnp.full((16, B), jnp.inf, F32)
        for s in range(NF):
            hit = jnp.where(ids == pat[ctx * NB + b, 4 + s], 0.0, hit)
        fb[:, b * B:(b + 1) * B] = hit

    @pl.when(ctx == 0)
    def _():
        kb[:, :EDGE, :] = jnp.zeros((H, EDGE, D), BF)
        vb[:, :EDGE, :] = jnp.zeros((H, EDGE, D), BF)

    @pl.when(ctx == 31)
    def _():
        back_r[...] = jnp.zeros((2, H, EDGE, D), BF)

    pl.semaphore_wait(barrier, len(peers))

    arrays = ((k_in, kb, EDGE), (v_in, vb, EDGE), (q_in, qb, 0), (g_in, gb, 0))

    def lanes(group, h):
        return pl.ds(pl.multiple_of((group * H + h) * D, D), D)

    def a_start(h):
        for n, (src, dst, base) in enumerate(arrays):
            place = dst.at[h, pl.ds(pl.multiple_of(base + z * R, 64), R), :]
            for d in (2, 1, 3):
                to = (z + d) % Z
                remote(src.at[:, lanes(to, h)], place, a_s.at[n, h], a_r.at[n, h], at(ctx, to)).start()
            pltpu.make_async_copy(src.at[:, lanes(z, h)], place, a_r.at[n, h]).start()

    def b_stage(h):
        done(kb.at[h, EDGE:, :], a_r.at[0, h])
        done(vb.at[h, EDGE:, :], a_r.at[1, h])

        @pl.when(ctx < 31)
        def _():
            remote(kb.at[h, W - EDGE:, :], kb.at[h, :EDGE, :], h_s.at[0, h], h_r.at[0, h], at(up, z)).start()
            remote(vb.at[h, W - EDGE:, :], vb.at[h, :EDGE, :], h_s.at[1, h], h_r.at[1, h], at(up, z)).start()

        ks = jnp.zeros((B, D), BF)
        vs = jnp.zeros((B, D), BF)
        for b in range(NB):
            r = slice(EDGE + b * B, EDGE + (b + 1) * B)
            ks = jnp.where(own == b, kb[h, r, :], ks)
            vs = jnp.where(own == b, vb[h, r, :], vs)
        rows[h, y, c] = jnp.where(c == 0, ks, vs)
        slot[h] = jnp.where(c == 0, vs, ks)
        remote(slot.at[h], rows.at[h, y, c], s1_s.at[h], s1_r.at[h], at(sib, z)).start()

    def c_stage(h):
        done(slot.at[h], s1_r.at[h])
        for d in (2, 1, 3):
            remote(rows.at[h, y], rows.at[h, y], y1_s.at[h], y1_r.at[h], at(ypeer(d), z)).start()

    def d_stage(h):
        done(rows.at[h, :3], y1_r.at[h])
        for j in range(3):
            place = (phase + 16 * j) // NB
            blk = jnp.zeros((B, D), BF)
            for s in range(3 * j if j < 2 else 5, (3, 6, 8)[j]):
                blk = jnp.where(place == s, rows[h, s // 2, s % 2], blk)
            if j == 1:
                blk = jnp.where(place == 2, rows[h, 1, 0], blk)
            pool[h, c, 3 * x + j] = blk
        mine = pool.at[h, c, pl.ds(3 * x, 3)]
        for d in (2, 1, 3):
            remote(mine, mine, x1_s.at[h], x1_r.at[h], at(xpeer(d), z)).start()

    def e_stage(h):
        done(pool.at[h, c, :9], x1_r.at[h])
        remote(pool.at[h, c], pool.at[h, c], s2_s.at[h], s2_r.at[h], at(sib, z)).start()

    def f_stage(h):
        done(qb.at[h], a_r.at[2, h])
        done(gb.at[h], a_r.at[3, h])

        @pl.when(ctx > 0)
        def _():
            done(kb.at[h, :EDGE, :], h_r.at[0, h])
            done(vb.at[h, :EDGE, :], h_r.at[1, h])

        done(pool.at[h, 0], s2_r.at[h])

    tri = lax.broadcasted_iota(jnp.int32, (B, B), 0) <= lax.broadcasted_iota(jnp.int32, (B, B), 1)

    def near_off(w):
        return jnp.where(ctx * NB - 3 + w >= 0, 0.0, jnp.inf).astype(F32)

    def pass1(h):
        qt_s[...] = qb[h].T
        m_s[...] = jnp.full((1, T), -jnp.inf, F32)
        for i in range(NF):
            s = nn(pool[h, 0, i], qt_s[...])
            sf[i] = s
            m_s[...] = jnp.maximum(m_s[...], jnp.max(s, axis=0, keepdims=True) - fb[i:i + 1, :])
        for w in range(NW):
            lo, hi = near_span(w)
            s = nn(kb[h, w * B:(w + 1) * B, :], qt_s[:, lo:hi])
            if w >= 3:
                first = jnp.where(tri, s[:, :B], -jnp.inf)
                s = jnp.concatenate([first, s[:, B:]], 1) if hi - lo > B else first
            sn[w, :, :hi - lo] = s
            top = jnp.max(s, axis=0, keepdims=True)
            if w < 3:
                top = top - near_off(w)
            m_s[:, lo:hi] = jnp.maximum(m_s[:, lo:hi], top)

    def pass2(h):
        m = m_s[...]
        l_s[...] = jnp.zeros((1, T), F32)
        ot_s[...] = jnp.zeros((D, T), F32)
        for i in range(NF):
            e = jnp.exp2((sf[i] - (m + fb[i:i + 1, :])) * C2)
            l_s[...] += jnp.sum(e, axis=0, keepdims=True)
            e = e.astype(BF)
            ef[i] = e
            ot_s[...] += tn(pool[h, 1, i], e)
        for w in range(NW):
            lo, hi = near_span(w)
            ref = m[:, lo:hi]
            if w < 3:
                ref = ref + near_off(w)
            e = jnp.exp2((sn[w, :, :hi - lo] - ref) * C2)
            l_s[:, lo:hi] += jnp.sum(e, axis=0, keepdims=True)
            e = e.astype(BF)
            en[w, :, :hi - lo] = e
            ot_s[:, lo:hi] += tn(vb[h, w * B:(w + 1) * B, :], e)
        inv = 1.0 / l_s[...]
        ot = ot_s[...] * inv
        ob[h] = ot.T.astype(BF)
        gt = (gb[h].T.astype(F32) * inv).astype(BF)
        gt_s[...] = gt
        gs_s[...] = gt.T
        de_s[...] = jnp.sum(gt.astype(F32) * ot, axis=0, keepdims=True)

    def pass3(h):
        dqt_s[...] = jnp.zeros((D, T), F32)
        for i in range(NF):
            e = ef[i]
            dpool[h, 1, i] = nn(e, gs_s[...]).astype(BF)
            dp = nn(pool[h, 1, i], gt_s[...])
            ds = (e.astype(F32) * (dp - de_s[...])).astype(BF)
            dpool[h, 0, i] = (nn(ds, qb[h]) * SCALE).astype(BF)
            dqt_s[...] += tn(pool[h, 0, i], ds)
        for w in range(NW):
            lo, hi = near_span(w)
            r = slice(w * B, (w + 1) * B)
            e = en[w, :, :hi - lo]
            dv = nn(e, gs_s[lo:hi, :])
            dp = nn(vb[h, r, :], gt_s[:, lo:hi])
            ds = (e.astype(F32) * (dp - de_s[:, lo:hi])).astype(BF)
            dk = nn(ds, qb[h, lo:hi, :]) * SCALE
            if w < 3:
                back_s[0, h, r, :] = dk.astype(BF)
                back_s[1, h, r, :] = dv.astype(BF)
            else:
                r = slice((w - 3) * B, (w - 2) * B)
                dkw[h, r, :] = dk
                dvw[h, r, :] = dv
            dqt_s[:, lo:hi] += tn(kb[h, w * B:(w + 1) * B, :], ds)
        dqb[h] = (dqt_s[...].T * SCALE).astype(BF)

    outs = ((ob, o_out), (dqb, dq_out), (dkb, dk_out), (dvb, dv_out))

    def o_start(n, h):
        src, dst = outs[n]
        place = dst.at[:, lanes(z, h)]
        for d in (2, 1, 3):
            to = (z + d) % Z
            part = src.at[h, pl.ds(pl.multiple_of(to * R, 64), R), :]
            remote(part, place, o_s.at[n, h], o_r.at[n, h], at(ctx, to)).start()
        part = src.at[h, pl.ds(pl.multiple_of(z * R, 64), R), :]
        pltpu.make_async_copy(part, place, o_r.at[n, h]).start()

    def g0(h):
        remote(dpool.at[h, 1 - c], sib_r.at[h], gs_sd.at[h], gs_rc.at[h], at(sib, z)).start()

        @pl.when(ctx > 0)
        def _():
            for n in range(2):
                remote(back_s.at[n, h], back_r.at[n, h], b_s.at[n, h], b_r.at[n, h], at(down, z)).start()

        o_start(1, h)

    def g1(h):
        done(sib_r.at[h], gs_rc.at[h])
        for i in range(NF):
            pair[h, i] = (dpool[h, c, i].astype(F32) + sib_r[h, i].astype(F32)).astype(BF)
        for d in (2, 1, 3):
            to = (x + d) % 4
            remote(pair.at[h, pl.ds(3 * to, 3)], x_r.at[h, d - 1], gx_s.at[h], gx_rc.at[h], at(xpeer(d), z)).start()

    def g2(h):
        done(x_r.at[h], gx_rc.at[h])
        tot = []
        for j in range(3):
            t = pair[h, 3 * x + j].astype(F32)
            for d in range(3):
                t = t + x_r[h, d, j].astype(F32)
            tot.append(t)
        for s in range(8):
            t = jnp.zeros((B, D), F32)
            for j in range(3):
                if 16 * j <= s * NB + 5 and s * NB <= 16 * j + 15:
                    t = jnp.where((phase + 16 * j) // NB == s, tot[j], t)
            ysl[h, s // 2, s % 2] = t.astype(BF)
        for d in (2, 1, 3):
            to = (y + d) % 4
            remote(ysl.at[h, to], y_r.at[h, d - 1], gy_s.at[h], gy_rc.at[h], at(ypeer(d), z)).start()

    def g3(h):
        done(y_r.at[h], gy_rc.at[h])
        for dst, core in ((zown, c), (zs, 1 - c)):
            t = ysl[h, y, core].astype(F32)
            for d in range(3):
                t = t + y_r[h, d, core].astype(F32)
            dst[h] = t.astype(BF)
        remote(zs.at[h], z_r.at[h], gz_s.at[h], gz_rc.at[h], at(sib, z)).start()

    def g4(h):
        done(z_r.at[h], gz_rc.at[h])

        @pl.when(ctx < 31)
        def _():
            done(back_r.at[0, h], b_r.at[0, h])
            done(back_r.at[1, h], b_r.at[1, h])

        mine, other = zown[h].astype(F32), z_r[h].astype(F32)
        for n, (part, total, dst) in enumerate(
            ((jnp.where(c == 0, mine, other), dkw, dkb), (jnp.where(c == 0, other, mine), dvw, dvb))
        ):
            for b in range(NB):
                r = slice(b * B, (b + 1) * B)
                t = total[h, r, :] + jnp.where(own == b, part, 0.0)
                if b >= 3:
                    t = t + back_r[n, h, (b - 3) * B:(b - 2) * B, :].astype(F32)
                dst[h, r, :] = t.astype(BF)
        o_start(2, h)
        o_start(3, h)

    a_start(0)
    a_start(1)
    b_stage(0)
    c_stage(0)
    d_stage(0)
    e_stage(0)

    @pl.loop(0, H)
    def _(t):
        ahead = t + 1 < H
        after = t > 0

        @pl.when(t + 2 < H)
        def _():
            a_start(t + 2)

        @pl.when(ahead)
        def _():
            b_stage(t + 1)

        @pl.when(after)
        def _():
            g1(t - 1)

        f_stage(t)
        pass1(t)

        @pl.when(ahead)
        def _():
            c_stage(t + 1)

        @pl.when(after)
        def _():
            g2(t - 1)

        pass2(t)
        o_start(0, t)

        @pl.when(ahead)
        def _():
            d_stage(t + 1)

        @pl.when(after)
        def _():
            g3(t - 1)

        pass3(t)
        g0(t)

        @pl.when(ahead)
        def _():
            e_stage(t + 1)

        @pl.when(after)
        def _():
            g4(t - 1)

    g1(H - 1)
    g2(H - 1)
    g3(H - 1)
    g4(H - 1)

    @pl.loop(0, H)
    def _(h):
        for n in range(4):
            done(qb.at[h, :3 * R, :], a_s.at[n, h])
            done(qb.at[h, :3 * R, :], o_s.at[n, h])
            done(qb.at[h], o_r.at[n, h])
        done(slot.at[h], s1_s.at[h])
        done(rows.at[h, :3], y1_s.at[h])
        done(pool.at[h, 0, :9], x1_s.at[h])
        done(pool.at[h, 0], s2_s.at[h])
        done(sib_r.at[h], gs_sd.at[h])
        done(x_r.at[h], gx_s.at[h])
        done(y_r.at[h], gy_s.at[h])
        done(z_r.at[h], gz_s.at[h])

        @pl.when(ctx < 31)
        def _():
            done(back_r.at[0, h], h_s.at[0, h])
            done(back_r.at[0, h], h_s.at[1, h])

        @pl.when(ctx > 0)
        def _():
            done(back_r.at[0, h], b_s.at[0, h])
            done(back_r.at[0, h], b_s.at[1, h])


def per_device(queries, keys, values, grad_out, pattern):
    vm = pltpu.VMEM
    dma = pltpu.SemaphoreType.DMA
    return pl.pallas_call(
        kernel,
        out_shape=[jax.ShapeDtypeStruct((R, H * Z * D), BF)] * 4,
        in_specs=[pl.BlockSpec(memory_space=pl.ANY)] * 4 + [pl.BlockSpec(memory_space=pltpu.SMEM)],
        out_specs=[pl.BlockSpec(memory_space=pl.ANY)] * 4,
        scratch_shapes=[
            vm((H, W, D), BF), vm((H, W, D), BF), vm((H, T, D), BF), vm((H, T, D), BF),
            vm((H, B, D), BF), vm((H, 4, 2, B, D), BF), vm((H, 2, NF, B, D), BF),
            vm((H, T, D), BF), vm((H, T, D), BF), vm((H, T, D), F32), vm((H, T, D), F32),
            vm((H, T, D), BF), vm((H, T, D), BF), vm((2, H, EDGE, D), BF), vm((2, H, EDGE, D), BF),
            vm((H, 2, NF, B, D), BF), vm((H, NF, B, D), BF), vm((H, NF, B, D), BF),
            vm((H, 3, 3, B, D), BF), vm((H, 4, 2, B, D), BF), vm((H, 3, 2, B, D), BF),
            vm((H, B, D), BF), vm((H, B, D), BF), vm((H, B, D), BF),
            vm((16, T), F32), vm((NF, B, T), F32), vm((NW, B, 512), F32), vm((NF, B, T), BF), vm((NW, B, 512), BF),
            vm((1, T), F32), vm((1, T), F32), vm((D, T), F32), vm((D, T), F32),
            vm((D, T), BF), vm((T, D), BF), vm((1, T), F32), vm((D, T), BF),
            dma((4, H)), dma((4, H)), dma((2, H)), dma((2, H)), dma((H,)), dma((H,)), dma((H,)), dma((H,)),
            dma((H,)), dma((H,)), dma((H,)), dma((H,)),
            dma((4, H)), dma((4, H)), dma((H,)), dma((H,)), dma((H,)), dma((H,)), dma((H,)), dma((H,)),
            dma((H,)), dma((H,)), dma((2, H)), dma((2, H)),
        ],
        compiler_params=pltpu.CompilerParams(
            collective_id=0, has_side_effects=True, vmem_limit_bytes=58 * 1024 * 1024
        ),
    )(keys, values, queries, grad_out, pattern)


def solution(mesh):
    split = P(("ctx", "head"), None)
    return jax.shard_map(
        per_device, mesh=mesh, in_specs=(split,) * 4 + (P(),), out_specs=(split,) * 4, check_vma=False
    )
```

time: 279 us -> 131 us (0.47); the launches traced: 274 us -> 131 us
  waiting for transfers between devices: 142 us -> 0 us
  Pallas kernels: 35.7 us -> 123 us
  starting transfers between devices: 42.9 us -> 0 us
  local copies, waits for them, and re-layouts: 23.5 us -> 7.33 us
  between operations: 16.1 us -> 0.65 us
  other arithmetic: 13.7 us -> 0 us
    pallas_call x1, Pallas kernels: 35.7 us -> 123 us  [per_device(): pl.pallas_call(kernel, out_shape=[jax.ShapeDtypeStruct((R, H * Z * D), BF...]
    reduce_scatter x2 -> x0, waiting for transfers between devices: 52.9 us -> none  [the longest x1 44.8 us: per_device(): lax.psum_scatter(both, 'ctx', scatter_dimension=0, tiled=True, axis_index...]
    all_to_all x8 -> x0, waiting for transfers between devices: 45.1 us -> none  [the longest x4 23.6 us: per_device(): return (out(o), out(dq), out(dk), out(dv))]
    all_gather x2 -> x0, waiting for transfers between devices: 44.1 us -> none  [the longest x1 27.6 us: per_device(): lax.all_gather(slot, 'ctx', axis=0, tiled=True, axis_index_groups=ROW_GRO...]
    all_to_all x8 -> x0, starting transfers between devices: 33.8 us -> none  [the longest x4 17.7 us: per_device(): k, v, q, g = (a2a(keys), a2a(values), a2a(queries), a2a(grad_out))]
    all_to_all x8 -> x0, local copies, waits for them, and re-layouts: 11.2 us -> none  [the longest x4 6.2 us: per_device(): k, v, q, g = (a2a(keys), a2a(values), a2a(queries), a2a(grad_out))]
    ppermute x4 -> x0, starting transfers between devices: 8.96 us -> none  [shifted(): lax.ppermute(value, 'ctx', [(s, s + steps) for s in range(first, last)])]
    slice x8 -> x0, local copies, waits for them, and re-layouts: 7.91 us -> none  [the longest x1 3.88 us: per_device(): kp, vp = (pool[:, 0].reshape(NF * B, 512), pool[:, 1].reshape(NF * B, 512))]
  transfers between devices with their start and end apart: 16 -> 0, of which waited for: 11 -> 0; matrix products, arithmetic and copies ran while one was open for 9% -> 0% of each run, Pallas kernels for 0% -> 0%
where the time goes in v2:
time: 131 us
  Pallas kernels  123 us (94%)
  local copies, waits for them, and re-layouts  7.33 us (6%)
    pallas_call x1, Pallas kernels, per_device(): pl.pallas_call(kernel, out_shape=[jax.ShapeDtypeStruct((R, H * Z * D), BF...  123 us
    unnamed x11, local copies, waits for them, and re-layouts  7.33 us

profile of v2, /device:TPU:1, one launch (start us, length us, event | category | flops | bytes accessed | tf_op | source)
XLA Modules:
  0.0 130.7 jit_solution(12885052570932582864)
XLA Ops:
  0.6 1.5 %copy.9.pat = s32[192,16]{1,0:T(8,128)} copy(s32[192,16]{0,1:T(8,128)} %param.9) | data formatting | bytes 24576 | tf_op args[4]
  2.1 122.8 %shard_map.84 = (bf16[192,2048]{1,0:T(8,128)(2,1)}, bf16[192,2048]{1,0:T(8,128)(2,1)}, bf16[192,2048]{1,0:T(8,128)(2,1)}, bf16[192,2048]{1,0:T(8,128)(2,1)}) custom-call(bf16[192,2048]{1,0:T(8,128)(2,1)} %k_in.1, bf16[192,2048]{1,0:T(8,128)(2,1)} %v_in.1, bf16[192,2048]{1,0:T(8,128)(2,1)} %q_in.1, bf16[192,2048]{1,0:T(8,128)(2,1)} %g_in.1, s32[192,16]{1,0:T(8,128)} %copy.9.pat), custom_call_target="tpu_custom_call" | custom-call | tf_op jit(solution)/shard_map/pallas_call | solution.py:418
  124.9 0.0 copy-start.2
  124.9 2.2 %copy.14 = bf16[192,2048]{1,0:T(8,128)(2,1)} copy(bf16[192,2048]{1,0:T(8,128)(2,1)} %get-tuple-element.8) | data formatting | bytes 1572864
  127.0 0.0 copy-done.2
  127.0 0.0 copy-start.1
  127.0 0.9 copy.15
  127.9 0.5 copy-done.1
  128.4 0.0 copy-start
  128.4 0.9 copy.16
  129.3 0.5 copy-done
  129.9 0.9 copy.17
Async XLA Ops:
  124.9 2.2 %copy-start.2 = (bf16[192,2048]{1,0:T(8,128)(2,1)S(1)}, bf16[192,2048]{1,0:T(8,128)(2,1)}, u32[]{:S(2)}) copy-start(bf16[192,2048]{1,0:T(8,128)(2,1)} %get-tuple-element.9) | copy-start | bytes 2359300
  127.0 1.4 %copy-start.1 = (bf16[192,2048]{1,0:T(8,128)(2,1)S(1)}, bf16[192,2048]{1,0:T(8,128)(2,1)}, u32[]{:S(2)}) copy-start(bf16[192,2048]{1,0:T(8,128)(2,1)} %get-tuple-element.10) | copy-start | bytes 2359300
  128.4 1.4 %copy-start = (bf16[192,2048]{1,0:T(8,128)(2,1)S(1)}, bf16[192,2048]{1,0:T(8,128)(2,1)}, u32[]{:S(2)}) copy-start(bf16[192,2048]{1,0:T(8,128)(2,1)} %get-tuple-element.11) | copy-start | bytes 2359300

commit v3 on v2

--- a/solution.py
+++ b/solution.py
@@ -24,6 +24,8 @@
 SCALE = 1.0 / math.sqrt(D)
 C2 = math.log2(math.e) / math.sqrt(D)
 MESH = pl.DeviceIdType.MESH
+KV = (0, 1)
+QG = (2, 3)
 
 
 def tn(a, b):
@@ -43,10 +45,10 @@
     o_out, dq_out, dk_out, dv_out,
     kb, vb, qb, gb, slot, rows, pool,
     ob, dqb, dkw, dvw, dkb, dvb, back_s, back_r,
-    dpool, sib_r, pair, x_r, ysl, y_r, zs, z_r, zown,
+    dpool, sib_r, pair, x_r, ysl, y_r,
     fb, sf, sn, ef, en, m_s, l_s, ot_s, dqt_s, gt_s, gs_s, de_s, qt_s,
-    a_s, a_r, h_s, h_r, s1_s, s1_r, y1_s, y1_r, x1_s, x1_r, s2_s, s2_r,
-    o_s, o_r, gs_sd, gs_rc, gx_s, gx_rc, gy_s, gy_rc, gz_s, gz_rc, b_s, b_r,
+    a_s, a_r, h_s, h_r, y1_s, y1_r, x1_s, x1_r, s2_s, s2_r,
+    o_s, o_r, gs_sd, gs_rc, gx_s, gx_rc, gy_s, gy_rc, b_s, b_r,
 ):
     ctx = lax.axis_index("ctx")
     z = lax.axis_index("head")
@@ -60,8 +62,11 @@
     def xpeer(d):
         return ((x + d) % 4) * 8 + y * 2 + c
 
-    def ypeer(d):
-        return x * 8 + ((y + d) % 4) * 2 + c
+    def rowpeer(d, other):
+        return ((y + d) % 4) * 2 + (1 - c if other else c)
+
+    row_moves = [(d, other) for other in (0, 1) for d in (2, 1, 3)] + [(0, 1)]
+    me8 = y * 2 + c
 
     def at(ctx_, z_):
         return {"ctx": ctx_, "head": z_}
@@ -76,18 +81,18 @@
 
     barrier = pltpu.get_barrier_semaphore()
     peers = [at(ctx, (z + d) % Z) for d in (1, 2, 3)]
-    peers += [at(ypeer(d), z) for d in (1, 2, 3)] + [at(xpeer(d), z) for d in (1, 2, 3)]
-    peers += [at(sib, z), at(up, z), at(down, z)]
+    peers += [at(x * 8 + rowpeer(*m), z) for m in row_moves] + [at(xpeer(d), z) for d in (1, 2, 3)]
+    peers += [at(up, z), at(down, z)]
     for dev in peers:
         pl.semaphore_signal(barrier, inc=1, device_id=dev, device_id_type=MESH)
 
-    phase = pat[NB * 32 - 1, 4] % 16
+    phase = pat[4, NB * 32 - 1] % 16
     own = (phase - ctx * NB + 192) % 16
     ids = phase + 16 * lax.broadcasted_iota(jnp.int32, (16, B), 0)
     for b in range(NB):
         hit = jnp.full((16, B), jnp.inf, F32)
         for s in range(NF):
-            hit = jnp.where(ids == pat[ctx * NB + b, 4 + s], 0.0, hit)
+            hit = jnp.where(ids == pat[4 + s, ctx * NB + b], 0.0, hit)
         fb[:, b * B:(b + 1) * B] = hit
 
     @pl.when(ctx == 0)
@@ -106,8 +111,9 @@
     def lanes(group, h):
         return pl.ds(pl.multiple_of((group * H + h) * D, D), D)
 
-    def a_start(h):
-        for n, (src, dst, base) in enumerate(arrays):
+    def a_start(h, which):
+        for n in which:
+            src, dst, base = arrays[n]
             place = dst.at[h, pl.ds(pl.multiple_of(base + z * R, 64), R), :]
             for d in (2, 1, 3):
                 to = (z + d) % Z
@@ -129,24 +135,22 @@
             r = slice(EDGE + b * B, EDGE + (b + 1) * B)
             ks = jnp.where(own == b, kb[h, r, :], ks)
             vs = jnp.where(own == b, vb[h, r, :], vs)
-        rows[h, y, c] = jnp.where(c == 0, ks, vs)
+        rows[h, me8] = jnp.where(c == 0, ks, vs)
         slot[h] = jnp.where(c == 0, vs, ks)
-        remote(slot.at[h], rows.at[h, y, c], s1_s.at[h], s1_r.at[h], at(sib, z)).start()
-
-    def c_stage(h):
-        done(slot.at[h], s1_r.at[h])
-        for d in (2, 1, 3):
-            remote(rows.at[h, y], rows.at[h, y], y1_s.at[h], y1_r.at[h], at(ypeer(d), z)).start()
+        for d, other in row_moves:
+            src = slot.at[h] if other else rows.at[h, me8]
+            to = at(x * 8 + rowpeer(d, other), z)
+            remote(src, rows.at[h, me8], y1_s.at[h], y1_r.at[h], to).start()
 
     def d_stage(h):
-        done(rows.at[h, :3], y1_r.at[h])
+        done(rows.at[h, :7], y1_r.at[h])
         for j in range(3):
             place = (phase + 16 * j) // NB
             blk = jnp.zeros((B, D), BF)
             for s in range(3 * j if j < 2 else 5, (3, 6, 8)[j]):
-                blk = jnp.where(place == s, rows[h, s // 2, s % 2], blk)
+                blk = jnp.where(place == s, rows[h, s], blk)
             if j == 1:
-                blk = jnp.where(place == 2, rows[h, 1, 0], blk)
+                blk = jnp.where(place == 2, rows[h, 2], blk)
             pool[h, c, 3 * x + j] = blk
         mine = pool.at[h, c, pl.ds(3 * x, 3)]
         for d in (2, 1, 3):
@@ -165,6 +169,7 @@
             done(kb.at[h, :EDGE, :], h_r.at[0, h])
             done(vb.at[h, :EDGE, :], h_r.at[1, h])
 
+    def f2_stage(h):
         done(pool.at[h, 0], s2_r.at[h])
 
     tri = lax.broadcasted_iota(jnp.int32, (B, B), 0) <= lax.broadcasted_iota(jnp.int32, (B, B), 1)
@@ -172,13 +177,9 @@
     def near_off(w):
         return jnp.where(ctx * NB - 3 + w >= 0, 0.0, jnp.inf).astype(F32)
 
-    def pass1(h):
+    def near1(h):
         qt_s[...] = qb[h].T
         m_s[...] = jnp.full((1, T), -jnp.inf, F32)
-        for i in range(NF):
-            s = nn(pool[h, 0, i], qt_s[...])
-            sf[i] = s
-            m_s[...] = jnp.maximum(m_s[...], jnp.max(s, axis=0, keepdims=True) - fb[i:i + 1, :])
         for w in range(NW):
             lo, hi = near_span(w)
             s = nn(kb[h, w * B:(w + 1) * B, :], qt_s[:, lo:hi])
@@ -190,6 +191,12 @@
             if w < 3:
                 top = top - near_off(w)
             m_s[:, lo:hi] = jnp.maximum(m_s[:, lo:hi], top)
+
+    def far1(h):
+        for i in range(NF):
+            s = nn(pool[h, 0, i], qt_s[...])
+            sf[i] = s
+            m_s[...] = jnp.maximum(m_s[...], jnp.max(s, axis=0, keepdims=True) - fb[i:i + 1, :])
 
     def pass2(h):
         m = m_s[...]
@@ -219,7 +226,7 @@
         gs_s[...] = gt.T
         de_s[...] = jnp.sum(gt.astype(F32) * ot, axis=0, keepdims=True)
 
-    def pass3(h):
+    def far3(h):
         dqt_s[...] = jnp.zeros((D, T), F32)
         for i in range(NF):
             e = ef[i]
@@ -228,6 +235,8 @@
             ds = (e.astype(F32) * (dp - de_s[...])).astype(BF)
             dpool[h, 0, i] = (nn(ds, qb[h]) * SCALE).astype(BF)
             dqt_s[...] += tn(pool[h, 0, i], ds)
+
+    def near3(h):
         for w in range(NW):
             lo, hi = near_span(w)
             r = slice(w * B, (w + 1) * B)
@@ -258,9 +267,10 @@
         part = src.at[h, pl.ds(pl.multiple_of(z * R, 64), R), :]
         pltpu.make_async_copy(part, place, o_r.at[n, h]).start()
 
+    def sib_send(h):
+        remote(dpool.at[h, 1 - c], sib_r.at[h], gs_sd.at[h], gs_rc.at[h], at(sib, z)).start()
+
     def g0(h):
-        remote(dpool.at[h, 1 - c], sib_r.at[h], gs_sd.at[h], gs_rc.at[h], at(sib, z)).start()
-
         @pl.when(ctx > 0)
         def _():
             for n in range(2):
@@ -289,32 +299,24 @@
             for j in range(3):
                 if 16 * j <= s * NB + 5 and s * NB <= 16 * j + 15:
                     t = jnp.where((phase + 16 * j) // NB == s, tot[j], t)
-            ysl[h, s // 2, s % 2] = t.astype(BF)
-        for d in (2, 1, 3):
-            to = (y + d) % 4
-            remote(ysl.at[h, to], y_r.at[h, d - 1], gy_s.at[h], gy_rc.at[h], at(ypeer(d), z)).start()
+            ysl[h, s] = t.astype(BF)
+        for d, other in row_moves:
+            to = rowpeer(d, other)
+            remote(ysl.at[h, to], y_r.at[h, me8], gy_s.at[h], gy_rc.at[h], at(x * 8 + to, z)).start()
+        y_r[h, me8] = ysl[h, me8]
 
     def g3(h):
-        done(y_r.at[h], gy_rc.at[h])
-        for dst, core in ((zown, c), (zs, 1 - c)):
-            t = ysl[h, y, core].astype(F32)
-            for d in range(3):
-                t = t + y_r[h, d, core].astype(F32)
-            dst[h] = t.astype(BF)
-        remote(zs.at[h], z_r.at[h], gz_s.at[h], gz_rc.at[h], at(sib, z)).start()
-
-    def g4(h):
-        done(z_r.at[h], gz_rc.at[h])
+        done(y_r.at[h, :7], gy_rc.at[h])
 
         @pl.when(ctx < 31)
         def _():
             done(back_r.at[0, h], b_r.at[0, h])
             done(back_r.at[1, h], b_r.at[1, h])
 
-        mine, other = zown[h].astype(F32), z_r[h].astype(F32)
         for n, (part, total, dst) in enumerate(
-            ((jnp.where(c == 0, mine, other), dkw, dkb), (jnp.where(c == 0, other, mine), dvw, dvb))
+            ((y_r, dkw, dkb), (y_r, dvw, dvb))
         ):
+            part = part[h, n].astype(F32) + part[h, 2 + n].astype(F32) + part[h, 4 + n].astype(F32) + part[h, 6 + n].astype(F32)
             for b in range(NB):
                 r = slice(b * B, (b + 1) * B)
                 t = total[h, r, :] + jnp.where(own == b, part, 0.0)
@@ -324,67 +326,60 @@
         o_start(2, h)
         o_start(3, h)
 
-    a_start(0)
-    a_start(1)
+    for h, which in ((0, KV), (1, KV), (2, KV), (0, QG), (3, KV), (1, QG), (2, QG), (3, QG)):
+        a_start(h, which)
     b_stage(0)
-    c_stage(0)
+    b_stage(1)
     d_stage(0)
+    b_stage(2)
+    d_stage(1)
     e_stage(0)
+    d_stage(2)
 
     @pl.loop(0, H)
     def _(t):
-        ahead = t + 1 < H
-        after = t > 0
-
-        @pl.when(t + 2 < H)
-        def _():
-            a_start(t + 2)
-
-        @pl.when(ahead)
-        def _():
-            b_stage(t + 1)
-
-        @pl.when(after)
+        f_stage(t)
+        near1(t)
+
+        @pl.when(t >= 1)
         def _():
             g1(t - 1)
 
-        f_stage(t)
-        pass1(t)
-
-        @pl.when(ahead)
-        def _():
-            c_stage(t + 1)
-
-        @pl.when(after)
-        def _():
-            g2(t - 1)
+        f2_stage(t)
+        far1(t)
+
+        @pl.when(t == 0)
+        def _():
+            b_stage(3)
+
+        @pl.when(t + 1 < H)
+        def _():
+            e_stage(t + 1)
+
+        @pl.when(t >= 2)
+        def _():
+            g3(t - 2)
 
         pass2(t)
         o_start(0, t)
-
-        @pl.when(ahead)
-        def _():
-            d_stage(t + 1)
-
-        @pl.when(after)
-        def _():
-            g3(t - 1)
-
-        pass3(t)
+        far3(t)
+        sib_send(t)
+
+        @pl.when(t == 0)
+        def _():
+            d_stage(3)
+
+        @pl.when(t >= 1)
+        def _():
+            g2(t - 1)
+
+        near3(t)
         g0(t)
 
-        @pl.when(ahead)
-        def _():
-            e_stage(t + 1)
-
-        @pl.when(after)
-        def _():
-            g4(t - 1)
-
     g1(H - 1)
+    g3(H - 2)
     g2(H - 1)
     g3(H - 1)
-    g4(H - 1)
 
     @pl.loop(0, H)
     def _(h):
@@ -392,14 +387,12 @@
             done(qb.at[h, :3 * R, :], a_s.at[n, h])
             done(qb.at[h, :3 * R, :], o_s.at[n, h])
             done(qb.at[h], o_r.at[n, h])
-        done(slot.at[h], s1_s.at[h])
-        done(rows.at[h, :3], y1_s.at[h])
+        done(rows.at[h, :7], y1_s.at[h])
         done(pool.at[h, 0, :9], x1_s.at[h])
         done(pool.at[h, 0], s2_s.at[h])
         done(sib_r.at[h], gs_sd.at[h])
         done(x_r.at[h], gx_s.at[h])
-        done(y_r.at[h], gy_s.at[h])
-        done(z_r.at[h], gz_s.at[h])
+        done(y_r.at[h, :7], gy_s.at[h])
 
         @pl.when(ctx < 31)
         def _():
@@ -410,36 +403,66 @@
         def _():
             done(back_r.at[0, h], b_s.at[0, h])
             done(back_r.at[0, h], b_s.at[1, h])
+
+
+def settle(*refs):
+    src, dst, held, in_sem, out_sem = refs[:4], refs[4:8], refs[8], refs[9], refs[10]
+    half = R // 2
+    parts = [(n, slice(m * half, (m + 1) * half), 2 * n + m) for n in range(4) for m in range(2)]
+    ins = [pltpu.make_async_copy(src[n].at[r], held.at[n, r], in_sem.at[i]) for n, r, i in parts]
+    outs = [pltpu.make_async_copy(held.at[n, r], dst[n].at[r], out_sem.at[i]) for n, r, i in parts]
+    for copy in ins:
+        copy.start()
+    for first, second in zip(ins, outs):
+        first.wait()
+        second.start()
+    for copy in outs:
+        copy.wait()
+
+
+def finish(results):
+    return pl.pallas_call(
+        settle,
+        out_shape=[jax.ShapeDtypeStruct((R, H * Z * D), BF)] * 4,
+        in_specs=[pl.BlockSpec(memory_space=pl.ANY)] * 4,
+        out_specs=[pl.BlockSpec(memory_space=pl.ANY)] * 4,
+        scratch_shapes=[
+            pltpu.VMEM((4, R, H * Z * D), BF),
+            pltpu.SemaphoreType.DMA((8,)),
+            pltpu.SemaphoreType.DMA((8,)),
+        ],
+        compiler_params=pltpu.CompilerParams(vmem_limit_bytes=58 * 1024 * 1024),
+    )(*results)
 
 
 def per_device(queries, keys, values, grad_out, pattern):
     vm = pltpu.VMEM
     dma = pltpu.SemaphoreType.DMA
-    return pl.pallas_call(
+    results = pl.pallas_call(
         kernel,
         out_shape=[jax.ShapeDtypeStruct((R, H * Z * D), BF)] * 4,
         in_specs=[pl.BlockSpec(memory_space=pl.ANY)] * 4 + [pl.BlockSpec(memory_space=pltpu.SMEM)],
         out_specs=[pl.BlockSpec(memory_space=pl.ANY)] * 4,
         scratch_shapes=[
             vm((H, W, D), BF), vm((H, W, D), BF), vm((H, T, D), BF), vm((H, T, D), BF),
-            vm((H, B, D), BF), vm((H, 4, 2, B, D), BF), vm((H, 2, NF, B, D), BF),
+            vm((H, B, D), BF), vm((H, 8, B, D), BF), vm((H, 2, NF, B, D), BF),
             vm((H, T, D), BF), vm((H, T, D), BF), vm((H, T, D), F32), vm((H, T, D), F32),
             vm((H, T, D), BF), vm((H, T, D), BF), vm((2, H, EDGE, D), BF), vm((2, H, EDGE, D), BF),
             vm((H, 2, NF, B, D), BF), vm((H, NF, B, D), BF), vm((H, NF, B, D), BF),
-            vm((H, 3, 3, B, D), BF), vm((H, 4, 2, B, D), BF), vm((H, 3, 2, B, D), BF),
-            vm((H, B, D), BF), vm((H, B, D), BF), vm((H, B, D), BF),
+            vm((H, 3, 3, B, D), BF), vm((H, 8, B, D), BF), vm((H, 8, B, D), BF),
             vm((16, T), F32), vm((NF, B, T), F32), vm((NW, B, 512), F32), vm((NF, B, T), BF), vm((NW, B, 512), BF),
             vm((1, T), F32), vm((1, T), F32), vm((D, T), F32), vm((D, T), F32),
             vm((D, T), BF), vm((T, D), BF), vm((1, T), F32), vm((D, T), BF),
             dma((4, H)), dma((4, H)), dma((2, H)), dma((2, H)), dma((H,)), dma((H,)), dma((H,)), dma((H,)),
-            dma((H,)), dma((H,)), dma((H,)), dma((H,)),
+            dma((H,)), dma((H,)),
             dma((4, H)), dma((4, H)), dma((H,)), dma((H,)), dma((H,)), dma((H,)), dma((H,)), dma((H,)),
-            dma((H,)), dma((H,)), dma((2, H)), dma((2, H)),
+            dma((2, H)), dma((2, H)),
         ],
         compiler_params=pltpu.CompilerParams(
             collective_id=0, has_side_effects=True, vmem_limit_bytes=58 * 1024 * 1024
         ),
-    )(keys, values, queries, grad_out, pattern)
+    )(keys, values, queries, grad_out, pattern.T)
+    return finish(results)
 
 
 def solution(mesh):

time: 131 us -> 98.1 us (0.75)
  Pallas kernels: 123 us -> 96.6 us
  local copies, waits for them, and re-layouts: 7.33 us -> 0 us
    pallas_call x1, Pallas kernels: 123 us -> 93.8 us  [per_device(): pl.pallas_call(kernel, out_shape=[jax.ShapeDtypeStruct((R, H * Z * D), BF...]
    unnamed x11 -> x0, local copies, waits for them, and re-layouts: 7.33 us -> none
    pallas_call x0 -> x1, Pallas kernels: none -> 2.79 us  [finish(): pl.pallas_call(settle, out_shape=[jax.ShapeDtypeStruct((R, H * Z * D), BF...]
where the time goes in v3:
time: 98.1 us; the launch traced here: 97.3 us
  Pallas kernels  96.6 us (98%)
    pallas_call x1, Pallas kernels, per_device(): pl.pallas_call(kernel, out_shape=[jax.ShapeDtypeStruct((R, H * Z * D), BF...  93.8 us
    pallas_call x1, Pallas kernels, finish(): pl.pallas_call(settle, out_shape=[jax.ShapeDtypeStruct((R, H * Z * D), BF...  2.79 us

profile of v3, /device:TPU:1, one launch (start us, length us, event | category | flops | bytes accessed | tf_op | source)
XLA Modules:
  0.0 97.3 jit_solution(17886537999474333622)
XLA Ops:
  0.6 93.8 %shard_map.84 = (bf16[192,2048]{1,0:T(8,128)(2,1)}, bf16[192,2048]{1,0:T(8,128)(2,1)}, bf16[192,2048]{1,0:T(8,128)(2,1)}, bf16[192,2048]{1,0:T(8,128)(2,1)}) custom-call(bf16[192,2048]{1,0:T(8,128)(2,1)} %k_in.1, bf16[192,2048]{1,0:T(8,128)(2,1)} %v_in.1, bf16[192,2048]{1,0:T(8,128)(2,1)} %q_in.1, bf16[192,2048]{1,0:T(8,128)(2,1)} %g_in.1, s32[16,192]{1,0:T(8,128)} %bitcast.1), custom_call_target="tpu_custom_call" | custom-call | tf_op jit(solution)/shard_map/pallas_call | solution.py:441
  94.5 2.8 %shard_map.85 = (bf16[192,2048]{1,0:T(8,128)(2,1)}, bf16[192,2048]{1,0:T(8,128)(2,1)}, bf16[192,2048]{1,0:T(8,128)(2,1)}, bf16[192,2048]{1,0:T(8,128)(2,1)}) custom-call(bf16[192,2048]{1,0:T(8,128)(2,1)} %get-tuple-element.8.refs_0_, bf16[192,2048]{1,0:T(8,128)(2,1)} %get-tuple-element.9.refs_1_, bf16[192,2048]{1,0:T(8,128)(2,1)} %get-tuple-element.10.refs_2_, ...), custom_call_target="tpu_custom_call" | custom-call | tf_op jit(solution)/shard_map/pallas_call | solution.py:424

commit v4 on v3

--- a/solution.py
+++ b/solution.py
@@ -12,7 +12,6 @@
 B = 128
 NB = 6
 NF = 12
-NW = 9
 EDGE = 384
 T = 768
 W = 1152
@@ -36,17 +35,13 @@
     return jnp.dot(a, b, preferred_element_type=F32)
 
 
-def near_span(w):
-    return max(0, w - 3) * B, (min(NB - 1, w) + 1) * B
-
-
 def kernel(
     k_in, v_in, q_in, g_in, pat,
     o_out, dq_out, dk_out, dv_out,
     kb, vb, qb, gb, slot, rows, pool,
     ob, dqb, dkw, dvw, dkb, dvb, back_s, back_r,
     dpool, sib_r, pair, x_r, ysl, y_r,
-    fb, sf, sn, ef, en, m_s, l_s, ot_s, dqt_s, gt_s, gs_s, de_s, qt_s,
+    fb, sf, sn, ef, en, m_s, l_s, ot_s, dqt_s, gt_s, gs_s, de_s, qt_s, df, pm,
     a_s, a_r, h_s, h_r, y1_s, y1_r, x1_s, x1_r, s2_s, s2_r,
     o_s, o_r, gs_sd, gs_rc, gx_s, gx_rc, gy_s, gy_rc, b_s, b_r,
 ):
@@ -172,52 +167,51 @@
     def f2_stage(h):
         done(pool.at[h, 0], s2_r.at[h])
 
-    tri = lax.broadcasted_iota(jnp.int32, (B, B), 0) <= lax.broadcasted_iota(jnp.int32, (B, B), 1)
-
-    def near_off(w):
-        return jnp.where(ctx * NB - 3 + w >= 0, 0.0, jnp.inf).astype(F32)
+    def pair_cols(p):
+        return slice(p * 256, p * 256 + 256)
+
+    def pair_rows(p):
+        return slice(p * 256, p * 256 + 640)
+
+    def masks():
+        key = lax.broadcasted_iota(jnp.int32, (640, 256), 0)
+        query = lax.broadcasted_iota(jnp.int32, (640, 256), 1)
+        first = jnp.where(ctx == 0, EDGE, 0)
+        window = (key >= (query // B) * B) & (key <= query + EDGE)
+        for p in range(3):
+            pm[p] = jnp.where(window & (key + p * 256 >= first), 0.0, -jnp.inf)
 
     def near1(h):
         qt_s[...] = qb[h].T
-        m_s[...] = jnp.full((1, T), -jnp.inf, F32)
-        for w in range(NW):
-            lo, hi = near_span(w)
-            s = nn(kb[h, w * B:(w + 1) * B, :], qt_s[:, lo:hi])
-            if w >= 3:
-                first = jnp.where(tri, s[:, :B], -jnp.inf)
-                s = jnp.concatenate([first, s[:, B:]], 1) if hi - lo > B else first
-            sn[w, :, :hi - lo] = s
-            top = jnp.max(s, axis=0, keepdims=True)
-            if w < 3:
-                top = top - near_off(w)
-            m_s[:, lo:hi] = jnp.maximum(m_s[:, lo:hi], top)
+        for p in range(3):
+            s = nn(kb[h, pair_rows(p), :], qt_s[:, pair_cols(p)]) + pm[p]
+            sn[p] = s
+            m_s[:, pair_cols(p)] = jnp.max(s, axis=0, keepdims=True)
 
     def far1(h):
+        top = jnp.full((8, T), -jnp.inf, F32)
         for i in range(NF):
             s = nn(pool[h, 0, i], qt_s[...])
             sf[i] = s
-            m_s[...] = jnp.maximum(m_s[...], jnp.max(s, axis=0, keepdims=True) - fb[i:i + 1, :])
+            top = jnp.maximum(top, jnp.max(s.reshape(16, 8, T), axis=0) - fb[i:i + 1, :])
+        m_s[...] = jnp.maximum(m_s[...], jnp.max(top, axis=0, keepdims=True))
 
     def pass2(h):
         m = m_s[...]
-        l_s[...] = jnp.zeros((1, T), F32)
-        ot_s[...] = jnp.zeros((D, T), F32)
+        total = jnp.zeros((8, T), F32)
         for i in range(NF):
             e = jnp.exp2((sf[i] - (m + fb[i:i + 1, :])) * C2)
-            l_s[...] += jnp.sum(e, axis=0, keepdims=True)
+            total = total + jnp.sum(e.reshape(16, 8, T), axis=0)
+            ef[i] = e.astype(BF)
+        l_s[...] = jnp.sum(total, axis=0, keepdims=True)
+        ot_s[...] = tn(pool[h, 1].reshape(NF * B, D), ef[...].reshape(NF * B, T))
+        for p in range(3):
+            cols = pair_cols(p)
+            e = jnp.exp2((sn[p] - m[:, cols]) * C2)
+            l_s[:, cols] += jnp.sum(e, axis=0, keepdims=True)
             e = e.astype(BF)
-            ef[i] = e
-            ot_s[...] += tn(pool[h, 1, i], e)
-        for w in range(NW):
-            lo, hi = near_span(w)
-            ref = m[:, lo:hi]
-            if w < 3:
-                ref = ref + near_off(w)
-            e = jnp.exp2((sn[w, :, :hi - lo] - ref) * C2)
-            l_s[:, lo:hi] += jnp.sum(e, axis=0, keepdims=True)
-            e = e.astype(BF)
-            en[w, :, :hi - lo] = e
-            ot_s[:, lo:hi] += tn(vb[h, w * B:(w + 1) * B, :], e)
+            en[p] = e
+            ot_s[:, cols] += tn(vb[h, pair_rows(p), :], e)
         inv = 1.0 / l_s[...]
         ot = ot_s[...] * inv
         ob[h] = ot.T.astype(BF)
@@ -227,32 +221,26 @@
         de_s[...] = jnp.sum(gt.astype(F32) * ot, axis=0, keepdims=True)
 
     def far3(h):
-        dqt_s[...] = jnp.zeros((D, T), F32)
+        sf[...] = nn(pool[h, 1].reshape(NF * B, D), gt_s[...]).reshape(NF, B, T)
         for i in range(NF):
-            e = ef[i]
-            dpool[h, 1, i] = nn(e, gs_s[...]).astype(BF)
-            dp = nn(pool[h, 1, i], gt_s[...])
-            ds = (e.astype(F32) * (dp - de_s[...])).astype(BF)
-            dpool[h, 0, i] = (nn(ds, qb[h]) * SCALE).astype(BF)
-            dqt_s[...] += tn(pool[h, 0, i], ds)
+            df[i] = (ef[i].astype(F32) * (sf[i] - de_s[...])).astype(BF)
+        dpool[h, 1] = nn(ef[...].reshape(NF * B, T), gs_s[...]).astype(BF).reshape(NF, B, D)
+        dpool[h, 0] = (nn(df[...].reshape(NF * B, T), qb[h]) * SCALE).astype(BF).reshape(NF, B, D)
 
     def near3(h):
-        for w in range(NW):
-            lo, hi = near_span(w)
-            r = slice(w * B, (w + 1) * B)
-            e = en[w, :, :hi - lo]
-            dv = nn(e, gs_s[lo:hi, :])
-            dp = nn(vb[h, r, :], gt_s[:, lo:hi])
-            ds = (e.astype(F32) * (dp - de_s[:, lo:hi])).astype(BF)
-            dk = nn(ds, qb[h, lo:hi, :]) * SCALE
-            if w < 3:
-                back_s[0, h, r, :] = dk.astype(BF)
-                back_s[1, h, r, :] = dv.astype(BF)
-            else:
-                r = slice((w - 3) * B, (w - 2) * B)
-                dkw[h, r, :] = dk
-                dvw[h, r, :] = dv
-            dqt_s[:, lo:hi] += tn(kb[h, w * B:(w + 1) * B, :], ds)
+        dqt_s[...] = tn(pool[h, 0].reshape(NF * B, D), df[...].reshape(NF * B, T))
+        dkw[h] = jnp.zeros((W, D), F32)
+        dvw[h] = jnp.zeros((W, D), F32)
+        for p in range(3):
+            cols, r = pair_cols(p), pair_rows(p)
+            e = en[p]
+            dvw[h, r, :] += nn(e, gs_s[cols, :])
+            dp = nn(vb[h, r, :], gt_s[:, cols])
+            ds = (e.astype(F32) * (dp - de_s[:, cols])).astype(BF)
+            dkw[h, r, :] += nn(ds, qb[h, cols, :]) * SCALE
+            dqt_s[:, cols] += tn(kb[h, r, :], ds)
+        back_s[0, h] = dkw[h, :EDGE, :].astype(BF)
+        back_s[1, h] = dvw[h, :EDGE, :].astype(BF)
         dqb[h] = (dqt_s[...].T * SCALE).astype(BF)
 
     outs = ((ob, o_out), (dqb, dq_out), (dkb, dk_out), (dvb, dv_out))
@@ -319,7 +307,7 @@
             part = part[h, n].astype(F32) + part[h, 2 + n].astype(F32) + part[h, 4 + n].astype(F32) + part[h, 6 + n].astype(F32)
             for b in range(NB):
                 r = slice(b * B, (b + 1) * B)
-                t = total[h, r, :] + jnp.where(own == b, part, 0.0)
+                t = total[h, EDGE + b * B:EDGE + (b + 1) * B, :] + jnp.where(own == b, part, 0.0)
                 if b >= 3:
                     t = t + back_r[n, h, (b - 3) * B:(b - 2) * B, :].astype(F32)
                 dst[h, r, :] = t.astype(BF)
@@ -328,6 +316,7 @@
 
     for h, which in ((0, KV), (1, KV), (2, KV), (0, QG), (3, KV), (1, QG), (2, QG), (3, QG)):
         a_start(h, which)
+    masks()
     b_stage(0)
     b_stage(1)
     d_stage(0)
@@ -446,13 +435,14 @@
         scratch_shapes=[
             vm((H, W, D), BF), vm((H, W, D), BF), vm((H, T, D), BF), vm((H, T, D), BF),
             vm((H, B, D), BF), vm((H, 8, B, D), BF), vm((H, 2, NF, B, D), BF),
-            vm((H, T, D), BF), vm((H, T, D), BF), vm((H, T, D), F32), vm((H, T, D), F32),
+            vm((H, T, D), BF), vm((H, T, D), BF), vm((H, W, D), F32), vm((H, W, D), F32),
             vm((H, T, D), BF), vm((H, T, D), BF), vm((2, H, EDGE, D), BF), vm((2, H, EDGE, D), BF),
             vm((H, 2, NF, B, D), BF), vm((H, NF, B, D), BF), vm((H, NF, B, D), BF),
             vm((H, 3, 3, B, D), BF), vm((H, 8, B, D), BF), vm((H, 8, B, D), BF),
-            vm((16, T), F32), vm((NF, B, T), F32), vm((NW, B, 512), F32), vm((NF, B, T), BF), vm((NW, B, 512), BF),
+            vm((16, T), F32), vm((NF, B, T), F32), vm((3, 640, 256), F32), vm((NF, B, T), BF), vm((3, 640, 256), BF),
             vm((1, T), F32), vm((1, T), F32), vm((D, T), F32), vm((D, T), F32),
             vm((D, T), BF), vm((T, D), BF), vm((1, T), F32), vm((D, T), BF),
+            vm((NF, B, T), BF), vm((3, 640, 256), F32),
             dma((4, H)), dma((4, H)), dma((2, H)), dma((2, H)), dma((H,)), dma((H,)), dma((H,)), dma((H,)),
             dma((H,)), dma((H,)),
             dma((4, H)), dma((4, H)), dma((H,)), dma((H,)), dma((H,)), dma((H,)), dma((H,)), dma((H,)),

time: 98.1 us -> 94.6 us (0.964)
  Pallas kernels: 96.6 us -> 93.7 us
    pallas_call x1, Pallas kernels: 93.8 us -> 90.9 us  [per_device(): pl.pallas_call(kernel, out_shape=[jax.ShapeDtypeStruct((R, H * Z * D), BF...]
where the time goes in v4:
time: 94.6 us; the launch traced here: 94.4 us
  Pallas kernels  93.7 us (99%)
    pallas_call x1, Pallas kernels, per_device(): pl.pallas_call(kernel, out_shape=[jax.ShapeDtypeStruct((R, H * Z * D), BF...  90.9 us
    pallas_call x1, Pallas kernels, finish(): pl.pallas_call(settle, out_shape=[jax.ShapeDtypeStruct((R, H * Z * D), BF...  2.79 us

profile of v4, /device:TPU:1, one launch (start us, length us, event | category | flops | bytes accessed | tf_op | source)
XLA Modules:
  0.0 94.4 jit_solution(16901470207375641871)
XLA Ops:
  0.6 90.9 %shard_map.84 = (bf16[192,2048]{1,0:T(8,128)(2,1)}, bf16[192,2048]{1,0:T(8,128)(2,1)}, bf16[192,2048]{1,0:T(8,128)(2,1)}, bf16[192,2048]{1,0:T(8,128)(2,1)}) custom-call(bf16[192,2048]{1,0:T(8,128)(2,1)} %k_in.1, bf16[192,2048]{1,0:T(8,128)(2,1)} %v_in.1, bf16[192,2048]{1,0:T(8,128)(2,1)} %q_in.1, bf16[192,2048]{1,0:T(8,128)(2,1)} %g_in.1, s32[16,192]{1,0:T(8,128)} %bitcast.1), custom_call_target="tpu_custom_call" | custom-call | tf_op jit(solution)/shard_map/pallas_call | solution.py:430
  91.6 2.8 %shard_map.85 = (bf16[192,2048]{1,0:T(8,128)(2,1)}, bf16[192,2048]{1,0:T(8,128)(2,1)}, bf16[192,2048]{1,0:T(8,128)(2,1)}, bf16[192,2048]{1,0:T(8,128)(2,1)}) custom-call(bf16[192,2048]{1,0:T(8,128)(2,1)} %get-tuple-element.8.refs_0_, bf16[192,2048]{1,0:T(8,128)(2,1)} %get-tuple-element.9.refs_1_, bf16[192,2048]{1,0:T(8,128)(2,1)} %get-tuple-element.10.refs_2_, ...), custom_call_target="tpu_custom_call" | custom-call | tf_op jit(solution)/shard_map/pallas_call | solution.py:413

commit v5 on v4

--- a/solution.py
+++ b/solution.py
@@ -323,13 +323,16 @@
     b_stage(2)
     d_stage(1)
     e_stage(0)
-    d_stage(2)
 
     @pl.loop(0, H)
     def _(t):
         f_stage(t)
         near1(t)
 
+        @pl.when(t == 0)
+        def _():
+            d_stage(2)
+
         @pl.when(t >= 1)
         def _():
             g1(t - 1)
@@ -347,7 +350,11 @@
 
         @pl.when(t >= 2)
         def _():
-            g3(t - 2)
+            g2(t - 2)
+
+        @pl.when(t >= 3)
+        def _():
+            g3(t - 3)
 
         pass2(t)
         o_start(0, t)
@@ -358,14 +365,12 @@
         def _():
             d_stage(3)
 
-        @pl.when(t >= 1)
-        def _():
-            g2(t - 1)
-
         near3(t)
         g0(t)
 
     g1(H - 1)
+    g3(H - 3)
+    g2(H - 2)
     g3(H - 2)
     g2(H - 1)
     g3(H - 1)

time: 94.6 us -> 88.5 us (0.936)
  Pallas kernels: 93.7 us -> 87.6 us
    pallas_call x1, Pallas kernels: 90.9 us -> 84.9 us  [per_device(): pl.pallas_call(kernel, out_shape=[jax.ShapeDtypeStruct((R, H * Z * D), BF...]
where the time goes in v5:
time: 88.5 us; the launch traced here: 88.3 us
  Pallas kernels  87.6 us (99%)
    pallas_call x1, Pallas kernels, per_device(): pl.pallas_call(kernel, out_shape=[jax.ShapeDtypeStruct((R, H * Z * D), BF...  84.9 us
    pallas_call x1, Pallas kernels, finish(): pl.pallas_call(settle, out_shape=[jax.ShapeDtypeStruct((R, H * Z * D), BF...  2.79 us

profile of v5, /device:TPU:1, one launch (start us, length us, event | category | flops | bytes accessed | tf_op | source)
XLA Modules:
  0.0 88.3 jit_solution(9017537657953547871)
XLA Ops:
  0.6 84.9 %shard_map.84 = (bf16[192,2048]{1,0:T(8,128)(2,1)}, bf16[192,2048]{1,0:T(8,128)(2,1)}, bf16[192,2048]{1,0:T(8,128)(2,1)}, bf16[192,2048]{1,0:T(8,128)(2,1)}) custom-call(bf16[192,2048]{1,0:T(8,128)(2,1)} %k_in.1, bf16[192,2048]{1,0:T(8,128)(2,1)} %v_in.1, bf16[192,2048]{1,0:T(8,128)(2,1)} %q_in.1, bf16[192,2048]{1,0:T(8,128)(2,1)} %g_in.1, s32[16,192]{1,0:T(8,128)} %bitcast.1), custom_call_target="tpu_custom_call" | custom-call | tf_op jit(solution)/shard_map/pallas_call | solution.py:435
  85.5 2.8 %shard_map.85 = (bf16[192,2048]{1,0:T(8,128)(2,1)}, bf16[192,2048]{1,0:T(8,128)(2,1)}, bf16[192,2048]{1,0:T(8,128)(2,1)}, bf16[192,2048]{1,0:T(8,128)(2,1)}) custom-call(bf16[192,2048]{1,0:T(8,128)(2,1)} %get-tuple-element.8.refs_0_, bf16[192,2048]{1,0:T(8,128)(2,1)} %get-tuple-element.9.refs_1_, bf16[192,2048]{1,0:T(8,128)(2,1)} %get-tuple-element.10.refs_2_, ...), custom_call_target="tpu_custom_call" | custom-call | tf_op jit(solution)/shard_map/pallas_call | solution.py:418

commit v6 on v5

--- a/solution.py
+++ b/solution.py
@@ -348,16 +348,17 @@
         def _():
             e_stage(t + 1)
 
-        @pl.when(t >= 2)
-        def _():
-            g2(t - 2)
-
-        @pl.when(t >= 3)
-        def _():
-            g3(t - 3)
-
         pass2(t)
         o_start(0, t)
+
+        @pl.when(t >= 2)
+        def _():
+            g2(t - 2)
+
+        @pl.when(t >= 3)
+        def _():
+            g3(t - 3)
+
         far3(t)
         sib_send(t)
 

time: 88.5 us -> 88 us (level)
  no operation moved by 1% of the time
where the time goes in v6:
time: 88 us; the launch traced here: 87.8 us
  Pallas kernels  87.2 us (99%)
    pallas_call x1, Pallas kernels, per_device(): pl.pallas_call(kernel, out_shape=[jax.ShapeDtypeStruct((R, H * Z * D), BF...  84.4 us
    pallas_call x1, Pallas kernels, finish(): pl.pallas_call(settle, out_shape=[jax.ShapeDtypeStruct((R, H * Z * D), BF...  2.79 us

profile of v6, /device:TPU:1, one launch (start us, length us, event | category | flops | bytes accessed | tf_op | source)
XLA Modules:
  0.0 87.8 jit_solution(10431324244411822793)
XLA Ops:
  0.6 84.4 %shard_map.84 = (bf16[192,2048]{1,0:T(8,128)(2,1)}, bf16[192,2048]{1,0:T(8,128)(2,1)}, bf16[192,2048]{1,0:T(8,128)(2,1)}, bf16[192,2048]{1,0:T(8,128)(2,1)}) custom-call(bf16[192,2048]{1,0:T(8,128)(2,1)} %k_in.1, bf16[192,2048]{1,0:T(8,128)(2,1)} %v_in.1, bf16[192,2048]{1,0:T(8,128)(2,1)} %q_in.1, bf16[192,2048]{1,0:T(8,128)(2,1)} %g_in.1, s32[16,192]{1,0:T(8,128)} %bitcast.1), custom_call_target="tpu_custom_call" | custom-call | tf_op jit(solution)/shard_map/pallas_call | solution.py:436
  85.0 2.8 %shard_map.85 = (bf16[192,2048]{1,0:T(8,128)(2,1)}, bf16[192,2048]{1,0:T(8,128)(2,1)}, bf16[192,2048]{1,0:T(8,128)(2,1)}, bf16[192,2048]{1,0:T(8,128)(2,1)}) custom-call(bf16[192,2048]{1,0:T(8,128)(2,1)} %get-tuple-element.8.refs_0_, bf16[192,2048]{1,0:T(8,128)(2,1)} %get-tuple-element.9.refs_1_, bf16[192,2048]{1,0:T(8,128)(2,1)} %get-tuple-element.10.refs_2_, ...), custom_call_target="tpu_custom_call" | custom-call | tf_op jit(solution)/shard_map/pallas_call | solution.py:419
